TPU v7x, 128 devices: a whole 4x4x4 slice. The times are simulated.
128 devices in a mesh: row: 16 (over x, y), col: 8 (over z, core).
Axes of the slice: x: 4, y: 4, z: 4, core: 2. Of those that a mesh axis runs over, the one named last changes fastest.
Arguments:
- noise: float32 [320, 320, 320], P(None, 'row', 'col'), may hold values from -6 to 6
- owners: int32 [128, 800, 1], P(('row', 'col')), may hold values from 0 to 255; in each aligned block of 800 rows (0 to 799, 800 to 1599, ..., all dimensions but the last counted through in order) at most 4 rows name the same one
Outputs:
- arrived: float32 [128, 128, 2, 4, 3, 320], P(('row', 'col'))
Inputs may be any that keep to these rules, and one draw needn't show every extreme that they name: `owners`: among the blocks of one device no domain appears more than 4 times, and in every draw some domain appears exactly 4 times among one device's blocks.
All inputs are finite; a program needn't handle non-finite values.
Results may differ from a plain program's by a relative error of at most 0.0001.
Values sent between devices are 32-bit elements; how exact they have to be, the bound alone decides.
No kernel may reach another device: no remote copies, remote signals or barrier semaphores. Data moves between devices by JAX's collectives and lax.ppermute only.
A program may use at most 128 MiB of HBM per device.

v0:
```python
import math

import jax
import jax.numpy as jnp
from jax import lax
from jax.sharding import PartitionSpec as P

DOM_DEV = 2


spectral_gain = 6.0
highest = lax.Precision.HIGHEST


def wavenumber(index, total):
    signed = jnp.where(index < total // 2, index, index - total)
    return (signed.astype(jnp.float32) * (2.0 * math.pi / total), index == total // 2)


def kernel_of(kz, kx, ky, edge_z, edge_x, edge_y):
    ksquare = kx * kx + ky * ky + kz * kz
    edge = edge_z | edge_x | edge_y | (ksquare <= 0.0)
    safe = jnp.where(edge, 1.0, ksquare)
    return jnp.where(edge, 0.0, spectral_gain * safe ** (-0.75) / (1.0 + safe))


def tables(count):
    steps = lax.iota(jnp.int32, count)
    product = steps[:, None] * steps[None, :] % count
    angle = product.astype(jnp.float32) * (2.0 * math.pi / count)
    return (jnp.cos(angle), jnp.sin(angle))


def block_table(cosine, sine, sign, scale):
    upper = jnp.stack([cosine, sign * sine])
    lower = jnp.stack([-sign * sine, cosine])
    return jnp.stack([upper, lower]) * scale


def pass_middle(field, table):
    return jnp.einsum("pamc,pqmk->qakc", field, table, precision=highest)


def pass_last(field, table):
    return jnp.einsum("pabm,pqmk->qabk", field, table, precision=highest)


def local(noise, owners):
    count = noise.shape[0]
    cosine, sine = tables(count)
    inverse_scale = 1.0 / count
    forward_table = block_table(cosine, sine, -1.0, 1.0)
    inverse_table = block_table(cosine, sine, 1.0, inverse_scale)
    opening = jnp.concatenate([cosine, -sine], axis=0)
    spectrum = jnp.dot(opening, noise.reshape(count, -1), precision=highest)
    spectrum = spectrum.reshape((2,) + noise.shape)
    spectrum = lax.all_to_all(spectrum, "col", split_axis=1, concat_axis=3, tiled=True)
    spectrum = pass_last(spectrum, forward_table)
    spectrum = lax.all_to_all(spectrum, "row", split_axis=3, concat_axis=2, tiled=True)
    spectrum = pass_middle(spectrum, forward_table)
    depth_z = spectrum.shape[1]
    depth_y = spectrum.shape[3]
    index_z = lax.axis_index("col") * depth_z + lax.iota(jnp.int32, depth_z)
    index_x = lax.iota(jnp.int32, count)
    index_y = lax.axis_index("row") * depth_y + lax.iota(jnp.int32, depth_y)
    kz, edge_z = wavenumber(index_z, count)
    kx, edge_x = wavenumber(index_x, count)
    ky, edge_y = wavenumber(index_y, count)
    kz = kz[:, None, None]
    kx = kx[None, :, None]
    ky = ky[None, None, :]
    kernel = kernel_of(
        kz, kx, ky, edge_z[:, None, None], edge_x[None, :, None], edge_y[None, None, :]
    )
    weighted_real = kernel * spectrum[0]
    weighted_imag = kernel * spectrum[1]
    parts = [(-wave * weighted_imag, wave * weighted_real) for wave in (kx, ky, kz)]
    section = [pass_middle(jnp.stack(pr), inverse_table) for pr in parts]
    moved = (
        lax.all_to_all(section[0], "row", split_axis=2, concat_axis=3, tiled=True),
        lax.all_to_all(section[1], "row", split_axis=2, concat_axis=3, tiled=True),
        lax.all_to_all(section[2], "row", split_axis=2, concat_axis=3, tiled=True),
    )
    section = [pass_last(item, inverse_table) for item in moved]
    moved = (
        lax.all_to_all(section[0], "col", split_axis=3, concat_axis=1, tiled=True),
        lax.all_to_all(section[1], "col", split_axis=3, concat_axis=1, tiled=True),
        lax.all_to_all(section[2], "col", split_axis=3, concat_axis=1, tiled=True),
    )
    real_table = inverse_table[:, 0]
    fields = [jnp.einsum("pmxy,pmk->kxy", item, real_table, precision=highest) for item in moved]
    psi = jnp.stack(fields)
    blocks_x = psi.shape[2]
    blocks_y = psi.shape[3]
    block_count = blocks_x * blocks_y
    payload = psi.reshape(3, count, block_count).transpose(2, 0, 1)
    nrow = lax.axis_size("row")
    ncol = lax.axis_size("col")
    devices = nrow * ncol
    domains = DOM_DEV * devices
    capacity = max(2, 3 * block_count // (2 * domains))
    owner = owners[0, :, 0]
    onehot = (owner[:, None] == lax.iota(jnp.int32, domains)[None, :]).astype(jnp.int32)
    ranks = jnp.cumsum(onehot, axis=0) - 1
    slot = jnp.sum(ranks * onehot, axis=1)
    target = owner * capacity + slot
    buffer = jnp.zeros((domains * capacity, 3, count), jnp.float32).at[target].set(payload)
    outgoing = buffer.reshape(devices, DOM_DEV, capacity, 3, count)
    arrived = lax.all_to_all(outgoing, ("row", "col"), split_axis=0, concat_axis=0, tiled=True)
    return arrived[None]


def solution(mesh):
    in_specs = (P(None, "row", "col"), P(("row", "col"), None, None))
    out_specs = P(("row", "col"), None, None, None, None, None)
    return jax.shard_map(local, mesh=mesh, in_specs=in_specs, out_specs=out_specs, check_vma=False)
```

profile of v0, /device:TPU:0, one launch (start us, length us, event | category | flops | bytes accessed | tf_op | source)
XLA Modules:
  0.0 901.5 jit_solution(13309821251448944628)
XLA Ops:
  16.2 14.1 %reshape.334 = f32[8,1,64000]{2,1,0:T(1,128)} reshape(f32[320,20,2,40]{3,2,1,0:T(2,128)} %bitcast.223) | data formatting | bytes 4096000
  41.2 21.2 %all-to-all-done = f32[8,1,64000]{2,1,0:T(1,128)} async-done(((f32[8,1,64000]{2,1,0:T(1,128)}), f32[8,1,64000]{2,1,0:T(1,128)}, u32[]{:S(2)}, u32[]{:S(2)}) %all-to-all-start) | async-done | bytes 2048032 | tf_op jit(solution)/shard_map/all_to_all | solution.py:57
  71.4 16.2 %reshape.335 = f32[320,20,2,40]{3,2,1,0:T(2,128)} reshape(f32[8,64000]{1,0:T(8,128)} %reduce.3) | data formatting | bytes 4096000
  87.6 9.3 %copy.219 = f32[2,8,40,20,40]{4,1,2,0,3:T(8,128)} copy(f32[2,8,40,20,40]{4,0,3,2,1:T(2,128)} %bitcast.224) | data formatting | bytes 4096000 | tf_op jit(solution)/shard_map/all_to_all | solution.py:57
  120.6 13.6 %reshape.336 = f32[16,1,32000]{2,1,0:T(1,128)} reshape(f32[320,20,2,40]{3,2,1,0:T(2,128)} %bitcast.226) | data formatting | bytes 4096000
  144.6 26.1 %all-to-all-done.1 = f32[16,1,32000]{2,1,0:T(1,128)} async-done(((f32[16,1,32000]{2,1,0:T(1,128)}), f32[16,1,32000]{2,1,0:T(1,128)}, u32[]{:S(2)}, u32[]{:S(2)}) %all-to-all-start.1) | async-done | bytes 2048032 | tf_op jit(solution)/shard_map/all_to_all | solution.py:59
  179.1 14.3 %reshape.337 = f32[320,20,2,40]{3,2,1,0:T(2,128)} reshape(f32[16,32000]{1,0:T(8,128)} %reduce.4) | data formatting | bytes 4096000
  201.2 9.1 %copy.111 = f32[2,40,320,20]{2,1,0,3:T(8,128)} copy(f32[2,40,320,20]{1,0,3,2:T(2,128)} %bitcast.228) | data formatting | bytes 4096000 | tf_op jit(solution)/shard_map/all_to_all | solution.py:59
  238.4 13.4 %reshape.338 = f32[16,1,32000]{2,1,0:T(1,128)} reshape(f32[320,20,2,40]{3,2,1,0:T(2,128)} %bitcast.229) | data formatting | bytes 4096000
  273.7 13.4 %reshape.346 = f32[16,1,32000]{2,1,0:T(1,128)} reshape(f32[320,20,2,40]{3,2,1,0:T(2,128)} %bitcast.230) | data formatting | bytes 4096000
  312.0 13.4 %reshape.342 = f32[16,1,32000]{2,1,0:T(1,128)} reshape(f32[320,20,2,40]{3,2,1,0:T(2,128)} %bitcast.231) | data formatting | bytes 4096000
  341.7 14.3 %reshape.347 = f32[320,20,2,40]{3,2,1,0:T(2,128)} reshape(f32[16,32000]{1,0:T(8,128)} %reduce.9) | data formatting | bytes 4096000
  356.0 9.2 %copy.115 = f32[2,40,20,16,20]{1,0,4,3,2:T(2,128)} copy(f32[2,40,20,16,20]{1,0,4,2,3:T(2,128)} %bitcast.232) | data formatting | bytes 4096000 | tf_op jit(solution)/shard_map/all_to_all | solution.py:80
  373.7 9.0 fusion.23
  391.3 14.1 %reshape.348 = f32[8,1,64000]{2,1,0:T(1,128)} reshape(f32[320,20,2,40]{3,2,1,0:T(2,128)} %bitcast.234) | data formatting | bytes 4096000
  418.1 14.3 %reshape.343 = f32[320,20,2,40]{3,2,1,0:T(2,128)} reshape(f32[16,32000]{1,0:T(8,128)} %reduce.7) | data formatting | bytes 4096000
  432.4 9.2 %copy.125 = f32[2,40,20,16,20]{1,0,4,3,2:T(2,128)} copy(f32[2,40,20,16,20]{1,0,4,2,3:T(2,128)} %bitcast.235) | data formatting | bytes 4096000 | tf_op jit(solution)/shard_map/all_to_all | solution.py:81
  450.1 9.2 %fusion.29 = f32[2,40,20,320]{3,1,2,0:T(8,128)} fusion(f32[2,40,20,320]{3,1,0,2:T(8,128)} %copy.127, f32[2,2,320,320,1]{3,2,1,0,4:T(8,128)S(1)} %get-tuple-element.12), kind=kOutput, calls=%fused_computation.34 | convolution fusion | flops 3932160000 | bytes 5734400 | tf_op jit(solution)/shard_map/pabm,pqmk->qabk/dot_general | solution.py:45
  468.0 14.1 %reshape.344 = f32[8,1,64000]{2,1,0:T(1,128)} reshape(f32[320,20,2,40]{3,2,1,0:T(2,128)} %bitcast.237) | data formatting | bytes 4096000
  495.5 14.3 %reshape.339 = f32[320,20,2,40]{3,2,1,0:T(2,128)} reshape(f32[16,32000]{1,0:T(8,128)} %reduce.5) | data formatting | bytes 4096000
  509.8 9.2 %copy.135 = f32[2,40,20,16,20]{1,0,4,3,2:T(2,128)} copy(f32[2,40,20,16,20]{1,0,4,2,3:T(2,128)} %bitcast.238) | data formatting | bytes 4096000 | tf_op jit(solution)/shard_map/all_to_all | solution.py:82
  527.5 9.0 fusion.35
  545.1 14.1 %reshape.340 = f32[8,1,64000]{2,1,0:T(1,128)} reshape(f32[320,20,2,40]{3,2,1,0:T(2,128)} %bitcast.240) | data formatting | bytes 4096000
  572.6 14.6 %reshape.349 = f32[320,20,2,40]{3,2,1,0:T(2,128)} reshape(f32[8,64000]{1,0:T(8,128)S(1)} %reduce.10) | data formatting | bytes 4096000
  587.2 9.4 %copy.218 = f32[2,40,20,8,40]{1,3,4,2,0:T(8,128)} copy(f32[2,40,20,8,40]{1,0,2,4,3:T(2,128)} %bitcast.241) | data formatting | bytes 4096000 | tf_op jit(solution)/shard_map/all_to_all | solution.py:86
  609.9 14.2 %reshape.345 = f32[320,20,2,40]{3,2,1,0:T(2,128)} reshape(f32[8,64000]{1,0:T(8,128)S(1)} %reduce.8) | data formatting | bytes 4096000
  624.1 9.5 %copy.217 = f32[2,40,20,8,40]{1,3,4,2,0:T(8,128)} copy(f32[2,40,20,8,40]{1,0,2,4,3:T(2,128)} %bitcast.243) | data formatting | bytes 4096000 | tf_op jit(solution)/shard_map/all_to_all | solution.py:87
  639.9 8.9 convolution_bitcast_fusion.3
  665.9 15.9 %reshape.341 = f32[320,20,2,40]{3,2,1,0:T(2,128)} reshape(f32[8,64000]{1,0:T(8,128)} %reduce.6) | data formatting | bytes 4096000
  681.8 9.3 %copy.216 = f32[2,40,20,8,40]{1,3,4,2,0:T(8,128)} copy(f32[2,40,20,8,40]{1,0,2,4,3:T(2,128)} %bitcast.245) | data formatting | bytes 4096000 | tf_op jit(solution)/shard_map/all_to_all | solution.py:88
  718.2 103.2 %scatter_fusion = f32[1024,3,320]{2,1,0:T(4,128)} fusion(f32[1024,3,320]{2,1,0:T(4,128)} %broadcast_in_dim.8, s32[800]{0:T(1024)S(1)} %fusion.73, f32[800,3,320]{2,1,0:T(4,128)} %copy.142), kind=kCustom, calls=%fused_computation | custom fusion | bytes 9219200 | tf_op jit(solution)/shard_map/scatter | solution.py:107
  825.4 69.5 %all_to_all.149 = f32[128,2,4,3,320]{4,2,3,1,0:T(4,128)} all-to-all(f32[128,2,4,3,320]{4,2,3,1,0:T(4,128)S(1)} %copy.143), channel_id=1, replica_groups=mesh['row'=16,'col'=8] {'row','col'}, dimensions={0} | all-to-all | bytes 7864320 | tf_op jit(solution)/shard_map/all_to_all | solution.py:109
  (94 shorter events, 342.6 us)
Async XLA Ops:
  0.0 2.1 copy-start
  30.2 32.2 %all-to-all-start = ((f32[8,1,64000]{2,1,0:T(1,128)}), f32[8,1,64000]{2,1,0:T(1,128)}, u32[]{:S(2)}, u32[]{:S(2)}) async-start(f32[8,1,64000]{2,1,0:T(1,128)} %reshape.334), calls=%async_computation | async-start | bytes 4096000 | tf_op jit(solution)/shard_map/all_to_all | solution.py:57
  41.2 61.9 %copy-start.4 = (f32[1,2,320,320]{3,2,0,1:T(8,128)}, f32[1,2,320,320]{3,2,0,1:T(8,128)S(1)}, u32[]{:S(2)}) copy-start(f32[1,2,320,320]{3,2,0,1:T(8,128)S(1)} %get-tuple-element.17) | copy-start | bytes 2457604
  134.2 36.5 %all-to-all-start.1 = ((f32[16,1,32000]{2,1,0:T(1,128)}), f32[16,1,32000]{2,1,0:T(1,128)}, u32[]{:S(2)}, u32[]{:S(2)}) async-start(f32[16,1,32000]{2,1,0:T(1,128)} %reshape.336), calls=%async_computation.1 | async-start | bytes 4096000 | tf_op jit(solution)/shard_map/all_to_all | solution.py:59
  251.9 35.3 %all-to-all-start.6 = ((f32[16,1,32000]{2,1,0:T(1,128)}), f32[16,1,32000]{2,1,0:T(1,128)}, u32[]{:S(2)}, u32[]{:S(2)}) async-start(f32[16,1,32000]{2,1,0:T(1,128)} %reshape.338), calls=%async_computation.6 | async-start | bytes 4096000 | tf_op jit(solution)/shard_map/all_to_all | solution.py:82
  287.1 38.3 %all-to-all-start.2 = ((f32[16,1,32000]{2,1,0:T(1,128)}), f32[16,1,32000]{2,1,0:T(1,128)}, u32[]{:S(2)}, u32[]{:S(2)}) async-start(f32[16,1,32000]{2,1,0:T(1,128)} %reshape.346), calls=%async_computation.2 | async-start | bytes 4096000 | tf_op jit(solution)/shard_map/all_to_all | solution.py:80
  325.4 79.9 %all-to-all-start.4 = ((f32[16,1,32000]{2,1,0:T(1,128)}), f32[16,1,32000]{2,1,0:T(1,128)}, u32[]{:S(2)}, u32[]{:S(2)}) async-start(f32[16,1,32000]{2,1,0:T(1,128)} %reshape.342), calls=%async_computation.4 | async-start | bytes 4096000 | tf_op jit(solution)/shard_map/all_to_all | solution.py:81
  405.4 76.7 %all-to-all-start.3 = ((f32[8,1,64000]{2,1,0:T(1,128)}), f32[8,1,64000]{2,1,0:T(1,128)}, u32[]{:S(2)}, u32[]{:S(2)}) async-start(f32[8,1,64000]{2,1,0:T(1,128)} %reshape.348), calls=%async_computation.3 | async-start | bytes 4096000 | tf_op jit(solution)/shard_map/all_to_all | solution.py:86
  482.0 4.8 copy-start.6
  482.1 77.1 %all-to-all-start.5 = ((f32[8,1,64000]{2,1,0:T(1,128)}), f32[8,1,64000]{2,1,0:T(1,128)}, u32[]{:S(2)}, u32[]{:S(2)}) async-start(f32[8,1,64000]{2,1,0:T(1,128)} %reshape.344), calls=%async_computation.5 | async-start | bytes 4096000 | tf_op jit(solution)/shard_map/all_to_all | solution.py:87
  559.2 98.3 %all-to-all-start.7 = ((f32[8,1,64000]{2,1,0:T(1,128)}), f32[8,1,64000]{2,1,0:T(1,128)}, u32[]{:S(2)}, u32[]{:S(2)}) async-start(f32[8,1,64000]{2,1,0:T(1,128)} %reshape.340), calls=%async_computation.7 | async-start | bytes 4096000 | tf_op jit(solution)/shard_map/all_to_all | solution.py:88
  633.6 6.3 copy-start.2
  639.9 9.0 copy-start.3
  697.4 8.9 copy-start.5
  894.8 6.5 copy-start.1
where the time goes:
time: 914 us; the launch traced here: 902 us
  local copies, waits for them, and re-layouts  554 us (61%)
  matrix products  102 us (11%)
  other arithmetic  81.8 us (9%)
  blocking collectives  69.5 us (8%)
  waiting for transfers between devices  47.3 us (5%)
  starting transfers between devices  46.2 us (5%)
    unnamed x30, local copies, waits for them, and re-layouts  228 us
    scatter x1, local copies, waits for them, and re-layouts, local(): jnp.zeros((domains * capacity, 3, count), jnp.float32).at[target]  103 us
    all_to_all x1, blocking collectives, local(): lax.all_to_all(outgoing, ('row', 'col'), split_axis=0, concat_axis=0, til...  69.5 us
    dot_general x4, matrix products, pass_last(): return jnp.einsum('pabm,pqmk->qabk', field, table, precision=highest)  36 us
    transpose x4, local copies, waits for them, and re-layouts, pass_last(): return jnp.einsum('pabm,pqmk->qabk', field, table, precision=highest)  34.5 us
    dot_general x4, matrix products, pass_middle(): return jnp.einsum('pamc,pqmk->qakc', field, table, precision=highest)  34.1 us
    dot_general x3, matrix products, local(): jnp.einsum('pmxy,pmk->kxy', item, real_table, precision=highest)  26.4 us
    all_to_all x1, waiting for transfers between devices, local(): lax.all_to_all(spectrum, 'row', split_axis=3, concat_axis=2, tiled=True)  26.1 us
  transfers between devices with their start and end apart: 8, of which 2 were waited for; matrix products, arithmetic and copies ran while one was open for 41% of the time, Pallas kernels for 0%

commit v1 on v0

v1 whole, which is shorter than its diff:
```python
import math

import jax
import jax.numpy as jnp
import ml_dtypes
import numpy as np
from jax import lax
from jax.experimental import pallas as pl
from jax.experimental.pallas import tpu as pltpu
from jax.sharding import Mesh
from jax.sharding import PartitionSpec as P

N = 320
GAIN = 6.0
ROWS, ZS, CORES = 16, 4, 2
CHIPS = ROWS * ZS
BU, BV = 20, 40
Q = 5
G = 7
LINES = BU * BV
EMPTY = G * 128
F32, BF16 = jnp.float32, jnp.bfloat16
STEP = 2.0 * math.pi / N


def basis():
    m = np.arange(N // 2)
    x = np.arange(N)
    angle = 2.0 * np.pi / N * (np.outer(m, x) % N)
    kw = (2.0 * np.pi / N * m)[:, None]
    weight = np.where(m == 0, 1.0, 2.0)[:, None] / N
    ana = np.zeros((N, N))
    syn = np.zeros((N, N))
    der = np.zeros((N, N))
    ana[0::2], ana[1::2] = np.cos(angle), np.sin(angle)
    syn[0::2], syn[1::2] = weight * np.cos(angle), weight * np.sin(angle)
    der[0::2], der[1::2] = -weight * kw * np.sin(angle), weight * kw * np.cos(angle)
    return ana, syn.T.copy(), der.T.copy()


def split_np(table):
    hi = table.astype(np.float32).astype(ml_dtypes.bfloat16)
    lo = (table - hi.astype(np.float64)).astype(np.float32).astype(ml_dtypes.bfloat16)
    return hi, lo


def lhs_table(table):
    hi, lo = split_np(table)
    return np.concatenate([hi, lo, hi], axis=1)


def rhs_table(table):
    hi, lo = split_np(table)
    return np.concatenate([hi, hi, lo], axis=0)


def make_tables():
    ana, syn, der = basis()
    third = np.arange(N)
    block, offset = third // BV, third % BV
    place = (block // 3) * 128 + (block % 3) * BV + offset
    first = ana.reshape(CHIPS, Q, N).transpose(1, 0, 2).reshape(N, N)
    t1 = np.zeros((384, 384))
    t1[place, :N] = ana.T
    a2 = np.zeros((N, 3, ROWS, 8))
    s3 = np.zeros((3, ROWS, G, N))
    d3 = np.zeros((3, ROWS, G, N))
    for i in range(3):
        for g in range(G):
            u = 3 * g + i
            if u < BU:
                at = np.arange(ROWS) * BU + u
                a2[:, i, :, g] = ana[:, at]
                s3[i, :, g] = syn[at]
                d3[i, :, g] = der[at]
    t4 = np.zeros((384, 384))
    t4[:N, place] = syn.T
    s5 = syn.reshape(N, CHIPS, Q).transpose(0, 2, 1).reshape(N, N)
    d5 = der.reshape(N, CHIPS, Q).transpose(0, 2, 1).reshape(N, N)
    m = np.arange(384) // 2
    kw = np.where(m < N // 2, 2.0 * np.pi / N * m, 0.0)
    even = np.arange(384) % 2 == 0
    swap = np.zeros((8, 384), np.float32)
    swap[0], swap[1] = np.where(even, kw, 0.0), np.where(even, 0.0, -kw)
    return dict(
        first=lhs_table(first),
        t1=rhs_table(t1),
        a2=lhs_table(a2.reshape(N, 384)),
        s3=lhs_table(s3.reshape(3 * ROWS * G, N)),
        d3=lhs_table(d3.reshape(3 * ROWS * G, N)),
        t4=rhs_table(t4),
        s5=lhs_table(s5),
        d5=lhs_table(d5),
        swap=swap,
    )


def split(value):
    hi = value.astype(BF16)
    return hi, (value - hi.astype(F32)).astype(BF16)


def rhs_split(value):
    hi, lo = split(value)
    return jnp.concatenate([hi, hi, lo], axis=0)


def lhs_split(value):
    hi, lo = split(value)
    return jnp.concatenate([hi, lo, hi], axis=1)


def dot(a, b):
    return jnp.dot(a, b, preferred_element_type=F32)


def dot_nt(a, b):
    return lax.dot_general(a, b, (((1,), (1,)), ((), ())), preferred_element_type=F32)


def column(row):
    return jnp.transpose(jnp.broadcast_to(row, (128, 128)))


def slot_codes(owner_ref):
    nb = 7
    lane = lax.broadcasted_iota(jnp.int32, (128, 128), 1)
    sub = lax.broadcasted_iota(jnp.int32, (128, 128), 0)
    one = lax.broadcasted_iota(jnp.int32, (1, 128), 1)
    rows = [owner_ref[:, b * 128 : (b + 1) * 128].astype(F32) for b in range(nb)]
    cols = [column(r) for r in rows]
    dests = []
    for b in range(nb):
        rank = jnp.sum(jnp.where((cols[b] == rows[b]) & (sub < lane), 1.0, 0.0), axis=0, keepdims=True)
        for e in range(b):
            rank = rank + jnp.sum(jnp.where(cols[e] == rows[b], 1.0, 0.0), axis=0, keepdims=True)
        owner = rows[b].astype(jnp.int32)
        device = owner >> 1
        dest = (device & 1) * (CHIPS * 8) + (device >> 1) * 8 + (owner & 1) * 4 + rank.astype(jnp.int32)
        dests.append(jnp.where(one + b * 128 < LINES, dest, -1).astype(F32))
    dcols = [column(d) for d in dests]
    values = []
    for b in range(nb):
        j = sub + b * 128
        group = jnp.zeros_like(j)
        for g in range(1, G):
            group = group + jnp.where(j >= g * 120, 1, 0)
        values.append((group * 8 + j - EMPTY).astype(F32))
    out = []
    for d in range(8):
        want = (lane + d * 128).astype(F32)
        total = jnp.zeros((128, 128), F32)
        for b in range(nb):
            total = total + jnp.where(dcols[b] == want, values[b], 0.0)
        out.append(jnp.sum(total, axis=0, keepdims=True) + float(EMPTY))
    return jnp.concatenate(out, axis=0)


def first_kernel(x_ref, owner_ref, table_ref, out_ref):
    codes = slot_codes(owner_ref)
    for j in range(CHIPS):
        out_ref[pl.ds(j * 48 + 40, 8), :] = codes
    parts = [x_ref[g * 120 : g * 120 + 128, :] for g in range(G - 1)]
    parts.append(x_ref[720:800, :])
    parts.append(jnp.zeros((48, N), F32))
    hi, lo = split(jnp.concatenate(parts, axis=0))
    th, tl = table_ref[:, 0:N], table_ref[:, N : 2 * N]
    y = dot_nt(th, hi) + (dot_nt(th, lo) + dot_nt(tl, hi))
    zero = jnp.zeros((CHIPS, 128), F32)
    for q in range(Q):
        for g in range(G):
            out_ref[pl.ds(q * 8 + g, CHIPS, stride=48), :] = y[q * CHIPS : (q + 1) * CHIPS, g * 128 : (g + 1) * 128]
        out_ref[pl.ds(q * 8 + G, CHIPS, stride=48), :] = zero


def middle_kernel(
    core_ref, own_ref, oth_ref, kern_ref, swap_ref, t1_ref, a2_ref, s3_ref, d3_ref, t4_ref,
    out_ref, u_ref, l4_ref, lines_ref, turn_ref,
):
    core = core_ref[0]
    mine = core == 0
    lane = lax.broadcasted_iota(jnp.int32, (1, 128), 1)

    pieces = []
    for z in range(ZS):
        a = own_ref[:, z, 0:40, :].reshape(ROWS * 40, 128)
        b = oth_ref[:, z, 0:40, :].reshape(ROWS * 40, 128)
        pieces.append(jnp.where(mine, a, b))
        pieces.append(jnp.where(mine, b, a))
    for i in range(3):
        cols = []
        for v in range(3):
            total = None
            for w in range(3):
                zc = 3 * v + w
                if zc >= 8:
                    continue
                shift = ((w - i) * BV) % 128
                moved = pltpu.roll(pieces[zc], shift, 1) if shift else pieces[zc]
                total = moved if total is None else jnp.where(lane >= w * BV, moved, total)
            cols.append(total)
        u_ref[i] = dot(lhs_split(jnp.concatenate(cols, axis=1)), t1_ref[...]).reshape(ROWS, Q, 8, 384)

    ca, cb = swap_ref[0:1, :], swap_ref[1:2, :]

    def plane(q, carry):
        parts = [u_ref[i, :, pl.ds(q, 1), :, :].reshape(ROWS * 8, 384) for i in range(3)]
        value = dot(a2_ref[...], rhs_split(jnp.concatenate(parts, axis=0))) * kern_ref[q]
        swapped = []
        for v in range(3):
            at = slice(v * 128, (v + 1) * 128)
            part = value[:, at]
            swapped.append(pltpu.roll(part, 127, 1) * ca[:, at] + pltpu.roll(part, 1, 1) * cb[:, at])
        plain = rhs_split(value)
        fields = (
            dot(d3_ref[...], plain),
            dot(s3_ref[...], rhs_split(jnp.concatenate(swapped, axis=1))),
            dot(s3_ref[...], plain),
        )
        for f in range(3):
            for i in range(3):
                for v in range(3):
                    part = fields[f][i * ROWS * G : (i + 1) * ROWS * G, v * 128 : (v + 1) * 128]
                    l4_ref[i, v, pl.ds(f * Q + q, ROWS * G, stride=16), :] = part
        return carry

    lax.fori_loop(0, Q, plane, 0)
    for i in range(3):
        for v in range(3):
            l4_ref[i, v, pl.ds(15, ROWS * G, stride=16), :] = jnp.zeros((ROWS * G, 128), F32)

    def rows4(r4, carry):
        ys = []
        for i in range(3):
            value = jnp.concatenate([l4_ref[i, v, pl.ds(r4 * 448, 448), :] for v in range(3)], axis=1)
            ys.append(dot(lhs_split(value), t4_ref[...]))
        for zc in range(8):
            v, w = zc // 3, zc % 3
            total = None
            for i in range(3):
                part = ys[i][:, v * 128 : (v + 1) * 128]
                shift = ((i - w) * BV) % 128
                part = pltpu.roll(part, shift, 1) if shift else part
                total = part if total is None else jnp.where(lane >= i * BV, part, total)
            lines_ref[zc] = total

        def one_row(rr, carry2):
            r = r4 * 4 + rr
            for zc in range(8):
                z, c = zc // 2, zc % 2
                blk = jnp.where(core == c, own_ref[r, z, 40:48, :], oth_ref[r, z, 40:48, :])
                code = jnp.where(mine, blk[0:4], blk[4:8]).astype(jnp.int32)
                for d in range(4):
                    idx = jnp.broadcast_to(code[d : d + 1], (16, 128))
                    at, group = idx & 127, idx >> 7
                    acc = jnp.zeros((16, 128), F32)
                    for g in range(G):
                        part = lines_ref[zc, pl.ds(rr * 112 + g * 16, 16), :]
                        acc = jnp.where(group == g, jnp.take_along_axis(part, at, axis=1), acc)
                    turn_ref[d, pl.ds(r * 8 + zc, 16, stride=128), :] = acc
            return carry2

        lax.fori_loop(0, 4, one_row, 0)
        return carry

    lax.fori_loop(0, 4, rows4, 0)

    def turned(pf, carry):
        for d in range(4):
            block = turn_ref[d, pl.ds(pf * 128, 128), :]
            out_ref[pl.ds(d * 2048 + pf, 128, stride=16), :] = jnp.transpose(block)
        return carry

    lax.fori_loop(0, 16, turned, 0)


def last_kernel(x_ref, s5_ref, d5_ref, out_ref):
    def load(slot, f):
        parts = [x_ref[pl.ds(slot * 16 + f * Q + q, CHIPS, stride=128), :] for q in range(Q)]
        return jnp.concatenate(parts, axis=0)

    def pair(k, carry):
        for e in range(2):
            slot = 2 * k + e
            both = rhs_split(jnp.concatenate([load(slot, 0), load(slot, 1)], axis=1))
            y = dot(s5_ref[...], both)
            out_ref[slot, 0] = y[:, 0:128]
            out_ref[slot, 1] = y[:, 128:256]
        both = rhs_split(jnp.concatenate([load(2 * k, 2), load(2 * k + 1, 2)], axis=1))
        y = dot(d5_ref[...], both)
        out_ref[2 * k, 2] = y[:, 0:128]
        out_ref[2 * k + 1, 2] = y[:, 128:256]
        return carry

    lax.fori_loop(0, 4, pair, 0)


VM = pl.BlockSpec(memory_space=pltpu.VMEM)
SM = pl.BlockSpec(memory_space=pltpu.SMEM)


def params(mib):
    return pltpu.CompilerParams(vmem_limit_bytes=mib * 2**20)


def first_call(x, owner, table):
    return pl.pallas_call(
        first_kernel,
        out_shape=jax.ShapeDtypeStruct((CHIPS * 48, 128), F32),
        in_specs=[VM] * 3,
        out_specs=VM,
        compiler_params=params(32),
    )(x, owner, table)


def middle_call(core, own, oth, kern, t):
    return pl.pallas_call(
        middle_kernel,
        out_shape=jax.ShapeDtypeStruct((CHIPS * 128, 128), F32),
        in_specs=[SM] + [VM] * 9,
        out_specs=VM,
        scratch_shapes=[
            pltpu.VMEM((3, ROWS, Q, 8, 384), F32),
            pltpu.VMEM((3, 3, ROWS * G * 16, 128), F32),
            pltpu.VMEM((8, 448, 128), F32),
            pltpu.VMEM((4, 16 * 128, 128), F32),
        ],
        compiler_params=params(56),
    )(core, own, oth, kern, t["swap"], t["t1"], t["a2"], t["s3"], t["d3"], t["t4"])


def last_call(x, s5, d5):
    return pl.pallas_call(
        last_kernel,
        out_shape=jax.ShapeDtypeStruct((8, 3, N, 128), F32),
        in_specs=[VM] * 3,
        out_specs=VM,
        compiler_params=params(32),
    )(x, s5, d5)


def filter_table(chip):
    def wave(p):
        return (p // 2).astype(F32) * STEP

    ka = wave(chip * Q + lax.iota(jnp.int32, Q))[:, None, None]
    kb = wave(lax.iota(jnp.int32, N))[None, :, None]
    kc = wave(lax.iota(jnp.int32, 384))[None, None, :]
    k2 = ka * ka + kb * kb + kc * kc
    off = (k2 <= 0.0) | (lax.iota(jnp.int32, 384)[None, None, :] >= N)
    safe = jnp.where(off, 1.0, k2)
    return jnp.where(off, 0.0, GAIN * safe ** (-0.75) / (1.0 + safe))


def local(noise, owners):
    t = make_tables()
    x = noise.transpose(1, 2, 0).reshape(LINES, N)
    owner = jnp.pad(owners.reshape(1, LINES), ((0, 0), (0, 896 - LINES)))
    sent = first_call(x, owner, t["first"]).reshape(CHIPS, 48, 128)
    own = lax.all_to_all(sent, ("row", "z"), split_axis=0, concat_axis=0, tiled=True)
    oth = lax.ppermute(own, "core", [(0, 1), (1, 0)])
    chip = lax.axis_index("row") * ZS + lax.axis_index("z")
    core = lax.axis_index("core").astype(jnp.int32).reshape(1)
    shape = (ROWS, ZS, 48, 128)
    slots = middle_call(core, own.reshape(shape), oth.reshape(shape), filter_table(chip), t)
    got = lax.all_to_all(slots.reshape(CHIPS, 128, 128), ("row", "z"), split_axis=0, concat_axis=0, tiled=True)
    out = last_call(got.reshape(CHIPS * 128, 128), t["s5"], t["d5"])
    return out.reshape(2, 4, 3, N, 128).transpose(4, 0, 1, 2, 3)[None]


def solution(mesh):
    fine = Mesh(mesh.devices.reshape(ROWS, ZS, CORES), ("row", "z", "core"))
    every = ("row", "z", "core")
    in_specs = (P(None, "row", ("z", "core")), P(every, None, None))
    out_specs = P(every, None, None, None, None, None)
    return jax.shard_map(local, mesh=fine, in_specs=in_specs, out_specs=out_specs, check_vma=False)
```

time: 914 us -> 152 us (0.17); the launches traced: 902 us -> 152 us
  local copies, waits for them, and re-layouts: 554 us -> 4.25 us
  matrix products: 102 us -> 0 us
  other arithmetic: 81.8 us -> 3.37 us
  Pallas kernels: 0 us -> 50.7 us
  waiting for transfers between devices: 47.3 us -> 0.02 us
  starting transfers between devices: 46.2 us -> 0.01 us
  blocking collectives: 69.5 us -> 93.2 us
    unnamed x30 -> x12, local copies, waits for them, and re-layouts: 228 us -> 3.56 us
    all_to_all x17 -> x0, local copies, waits for them, and re-layouts: 133 us -> none  [the longest x2 17.7 us: local(): lax.all_to_all(section[0], 'row', split_axis=2, concat_axis=3, tiled=True)]
    scatter x1 -> x0, local copies, waits for them, and re-layouts: 103 us -> none  [local(): jnp.zeros((domains * capacity, 3, count), jnp.float32).at[target]]
    dot_general x12 -> x0, matrix products: 102 us -> none  [the longest x4 36 us: pass_last(): return jnp.einsum('pabm,pqmk->qabk', field, table, precision=highest)]
    transpose x8 -> x0, local copies, waits for them, and re-layouts: 66.8 us -> none  [the longest x4 34.5 us: pass_last(): return jnp.einsum('pabm,pqmk->qabk', field, table, precision=highest)]
    all_to_all x8 -> x0, other arithmetic: 64.7 us -> none  [the longest x1 8.42 us: local(): lax.all_to_all(section[0], 'row', split_axis=2, concat_axis=3, tiled=True)]
    pallas_call x0 -> x3, Pallas kernels: none -> 50.7 us  [the longest x1 42.7 us: middle_call(): pl.pallas_call(middle_kernel, out_shape=jax.ShapeDtypeStruct((CHIPS * 128...]
    all_to_all x8 -> x0, waiting for transfers between devices: 47.3 us -> none  [the longest x1 26.1 us: local(): lax.all_to_all(spectrum, 'row', split_axis=3, concat_axis=2, tiled=True)]
  transfers between devices with their start and end apart: 8 -> 1, of which waited for: 2 -> 0; matrix products, arithmetic and copies ran while one was open for 41% -> 2% of each run, Pallas kernels for 0% -> 0%
where the time goes in v1:
time: 152 us
  blocking collectives  93.2 us (61%)
  Pallas kernels  50.7 us (33%)
  local copies, waits for them, and re-layouts  4.25 us (3%)
  other arithmetic  3.37 us (2%)
    all_to_all x1, blocking collectives, local(): lax.all_to_all(slots.reshape(CHIPS, 128, 128), ('row', 'z'), split_axis=0...  57.6 us
    pallas_call x1, Pallas kernels, middle_call(): pl.pallas_call(middle_kernel, out_shape=jax.ShapeDtypeStruct((CHIPS * 128...  42.7 us
    all_to_all x1, blocking collectives, local(): lax.all_to_all(sent, ('row', 'z'), split_axis=0, concat_axis=0, tiled=True)  35.5 us
    pallas_call x1, Pallas kernels, last_call(): pl.pallas_call(last_kernel, out_shape=jax.ShapeDtypeStruct((8, 3, N, 128)...  6.28 us
    unnamed x12, local copies, waits for them, and re-layouts  3.56 us
    select_n x1, other arithmetic, filter_table(): return jnp.where(off, 0.0, GAIN * safe ** (-0.75) / (1.0 + safe))  3.26 us
  transfers between devices with their start and end apart: 1, of which 0 were waited for; matrix products, arithmetic and copies ran while one was open for 2% of the time, Pallas kernels for 0%

profile of v1, /device:TPU:0, one launch (start us, length us, event | category | flops | bytes accessed | tf_op | source)
XLA Modules:
  0.0 151.5 jit_solution(11128760698922689592)
XLA Ops:
  0.0 0.7 pad.4.owner_ref
  0.7 0.0 copy-start
  0.7 1.3 copy-done
  2.0 0.0 copy-start.3
  2.0 1.1 copy-done.3
  3.1 1.7 %shard_map.109 = f32[3072,128]{1,0:T(8,128)S(1)} custom-call(f32[800,320]{1,0:T(8,128)S(1)} %bitcast.17, s32[1,896]{1,0:T(1,128)S(1)} %pad.4.owner_ref, bf16[320,960]{1,0:T(8,128)(2,1)S(1)} %copy-done.3), custom_call_target="tpu_custom_call" | custom-call | tf_op jit(solution)/shard_map/pallas_call | solution.py:307
  4.8 35.5 %all_to_all.10 = f32[64,48,128]{2,1,0:T(8,128)S(1)} all-to-all(f32[64,48,128]{2,1,0:T(8,128)S(1)} %bitcast.16), channel_id=1, replica_groups=mesh['row'=16,'z'=4,'core'=2] {'row','z'}, dimensions={0} | all-to-all | bytes 3145728 | tf_op jit(solution)/shard_map/all_to_all | solution.py:360
  40.3 0.0 copy-start.4
  40.3 0.0 collective-permute-start
  40.4 0.1 broadcast_add_fusion
  40.4 3.3 %fusion.4.kern_ref = f32[5,320,384]{2,1,0:T(8,128)} fusion(f32[384]{0:T(512)S(1)} %fusion.11, f32[5,320]{1,0:T(8,128)S(1)} %broadcast_add_fusion, pred[384]{0:T(512)(128)(4,1)S(1)} %iota_compare_fusion), kind=kLoop, calls=%fused_computation.6 | loop fusion | flops 4915200 | bytes 2465920 | tf_op jit(solution)/shard_map/jit(_where)/select_n | solution.py:352
  43.7 0.0 collective-permute-done
  43.7 0.0 copy-start.5
  43.7 0.0 copy-done.4
  43.7 1.2 copy-done.5
  44.9 42.7 %shard_map.110 = f32[8192,128]{1,0:T(8,128)} custom-call(s32[1]{0:T(128)} %bitcast.core_ref, f32[16,4,48,128]{3,2,1,0:T(8,128)} %bitcast.19, f32[16,4,48,128]{3,2,1,0:T(8,128)} %bitcast.20, f32[5,320,384]{2,1,0:T(8,128)} %fusion.4.kern_ref, f32[8,384]{1,0:T(8,128)} %constant.89.clone.swap_ref, bf16[1152,384]{1,0:T(8,128)(2,1)} %constant.90.clone.t1_ref, ...), custom_call_target="tpu_custom_call" | custom-call | tf_op jit(solution)/shard_map/pallas_call | solution.py:317
  87.6 0.0 copy-start.1
  87.6 0.0 copy-start.2
  87.6 57.6 %all_to_all.11 = f32[64,128,128]{2,1,0:T(8,128)S(1)} all-to-all(f32[64,128,128]{2,1,0:T(8,128)} %bitcast.18), channel_id=1, replica_groups=mesh['row'=16,'z'=4,'core'=2] {'row','z'}, dimensions={0} | all-to-all | bytes 8388608 | tf_op jit(solution)/shard_map/all_to_all | solution.py:366
  145.2 0.0 copy-done.1
  145.2 0.0 copy-done.2
  145.2 6.3 %shard_map.111 = f32[8,3,320,128]{3,2,1,0:T(8,128)} custom-call(f32[8192,128]{1,0:T(8,128)S(1)} %bitcast.15, bf16[320,960]{1,0:T(8,128)(2,1)S(1)} %copy-done.2, bf16[320,960]{1,0:T(8,128)(2,1)S(1)} %copy-done.1), custom_call_target="tpu_custom_call" | custom-call | tf_op jit(solution)/shard_map/pallas_call | solution.py:333
  (4 shorter events, 0.0 us)
Async XLA Ops:
  0.7 1.3 copy-start
  2.0 1.1 copy-start.3
  40.3 3.4 %copy-start.4 = (f32[64,48,128]{2,1,0:T(8,128)}, f32[64,48,128]{2,1,0:T(8,128)S(1)}, u32[]{:S(2)}) copy-start(f32[64,48,128]{2,1,0:T(8,128)S(1)} %all_to_all.10) | copy-start | bytes 4718596
  40.3 3.4 %collective-permute-start = (f32[64,48,128]{2,1,0:T(8,128)S(1)}, f32[64,48,128]{2,1,0:T(8,128)S(1)}, u32[]{:S(2)}, u32[]{:S(2)}) collective-permute-start(f32[64,48,128]{2,1,0:T(8,128)S(1)} %all_to_all.10), channel_id=1, source_target_pairs={{0,1},{1,0},{2,3},{3,2},{4,5},{5,4},{6,7},{7,6},{8,9},{9,8},{10,11... | collective-permute-start | bytes 4718600 | tf_op jit(solution)/shard_map/ppermute | solution.py:361
  43.7 1.2 copy-start.5
  87.6 57.6 %copy-start.1 = (bf16[320,960]{1,0:T(8,128)(2,1)S(1)}, bf16[320,960]{1,0:T(8,128)(2,1)}, u32[]{:S(2)}) copy-start(bf16[320,960]{1,0:T(8,128)(2,1)} %constant.96.clone.d5_ref) | copy-start | bytes 1843204
  87.6 57.6 %copy-start.2 = (bf16[320,960]{1,0:T(8,128)(2,1)S(1)}, bf16[320,960]{1,0:T(8,128)(2,1)}, u32[]{:S(2)}) copy-start(bf16[320,960]{1,0:T(8,128)(2,1)} %constant.95.clone.s5_ref) | copy-start | bytes 1843204

commit v2 on v1

v2 whole, which is shorter than its diff:
```python
import math

import jax
import jax.numpy as jnp
import ml_dtypes
import numpy as np
from jax import lax
from jax.experimental import pallas as pl
from jax.experimental.pallas import tpu as pltpu
from jax.sharding import Mesh
from jax.sharding import PartitionSpec as P

N = 320
GAIN = 6.0
ROWS, ZS, CORES = 16, 4, 2
CHIPS = ROWS * ZS
BU, BV = 20, 40
Q = 5
CH = 48
FQ = 3 * Q
G = 7
LINES = BU * BV
EMPTY = G * 128
F32, BF16 = jnp.float32, jnp.bfloat16
STEP = 2.0 * math.pi / N


def basis():
    m = np.arange(N // 2)
    x = np.arange(N)
    angle = 2.0 * np.pi / N * (np.outer(m, x) % N)
    kw = (2.0 * np.pi / N * m)[:, None]
    weight = np.where(m == 0, 1.0, 2.0)[:, None] / N
    ana = np.zeros((N, N))
    syn = np.zeros((N, N))
    der = np.zeros((N, N))
    ana[0::2], ana[1::2] = np.cos(angle), np.sin(angle)
    syn[0::2], syn[1::2] = weight * np.cos(angle), weight * np.sin(angle)
    der[0::2], der[1::2] = -weight * kw * np.sin(angle), weight * kw * np.cos(angle)
    return ana, syn.T.copy(), der.T.copy()


def split_np(table):
    hi = table.astype(np.float32).astype(ml_dtypes.bfloat16)
    lo = (table - hi.astype(np.float64)).astype(np.float32).astype(ml_dtypes.bfloat16)
    return hi, lo


def lhs_table(table):
    hi, lo = split_np(table)
    return np.concatenate([hi, lo, hi], axis=1)


def rhs_table(table):
    hi, lo = split_np(table)
    return np.concatenate([hi, hi, lo], axis=0)


def mix_table(table):
    hi, lo = split_np(table)
    return np.concatenate([hi[:256], hi[:256], lo[:256], hi[256:320], hi[256:320], lo[256:384]], axis=0)


def make_tables():
    ana, syn, der = basis()
    third = np.arange(N)
    block, offset = third // BV, third % BV
    places = [(block // 3) * 128 + ((block + i) % 3) * BV + offset for i in range(3)]
    first = ana.reshape(CHIPS, Q, N).transpose(1, 0, 2).reshape(N, N)
    t1 = np.zeros((3, 384, 384))
    t4 = np.zeros((3, 384, 384))
    for i in range(3):
        t1[i, places[i], :N] = ana.T
        t4[i][:N, places[i]] = syn.T
    a2 = np.zeros((N, 3, ROWS, 8))
    s3 = np.zeros((3, ROWS, 8, N))
    d3 = np.zeros((3, ROWS, 8, N))
    for i in range(3):
        for g in range(G):
            u = 3 * g + i
            if u < BU:
                at = np.arange(ROWS) * BU + u
                a2[:, i, :, g] = ana[:, at]
                s3[i, :, g] = syn[at]
                d3[i, :, g] = der[at]
    s5 = syn.reshape(N, CHIPS, Q).transpose(0, 2, 1).reshape(N, N)
    d5 = der.reshape(N, CHIPS, Q).transpose(0, 2, 1).reshape(N, N)
    m = np.arange(384) // 2
    kw = np.where(m < N // 2, 2.0 * np.pi / N * m, 0.0)
    even = np.arange(384) % 2 == 0
    swap = np.zeros((8, 384), np.float32)
    swap[0], swap[1] = np.where(even, kw, 0.0), np.where(even, 0.0, -kw)
    return dict(
        first=lhs_table(first),
        t1=np.stack([rhs_table(t) for t in t1]),
        a2=lhs_table(a2.reshape(N, 384)),
        s3=lhs_table(s3.reshape(384, N)),
        d3=lhs_table(d3.reshape(384, N)),
        t4=np.stack([mix_table(t) for t in t4]),
        s5=lhs_table(s5),
        d5=lhs_table(d5),
        swap=swap,
    )


def split(value):
    hi = value.astype(BF16)
    return hi, (value - hi.astype(F32)).astype(BF16)


def rhs_split(value):
    hi, lo = split(value)
    return jnp.concatenate([hi, hi, lo], axis=0)


def lhs_split(value):
    hi, lo = split(value)
    return jnp.concatenate([hi, lo, hi], axis=1)


def mix_split(value):
    hi, lo = split(value[:, :256])
    tail = value[:, 256:]
    tail_hi = tail.astype(BF16)
    moved = pltpu.roll(tail - tail_hi.astype(F32), 64, 1)
    lane = lax.broadcasted_iota(jnp.int32, (1, 128), 1)
    mixed = jnp.where(lane < 64, tail, moved).astype(BF16)
    return jnp.concatenate([hi, lo, hi, mixed, tail_hi], axis=1)


def dot(a, b):
    return jnp.dot(a, b, preferred_element_type=F32)


def dot_nt(a, b):
    return lax.dot_general(a, b, (((1,), (1,)), ((), ())), preferred_element_type=F32)


def column(row):
    return jnp.transpose(jnp.broadcast_to(row, (128, 128)))


def slot_codes(owner_ref, turn):
    nb = 7
    lane = lax.broadcasted_iota(jnp.int32, (128, 128), 1)
    sub = lax.broadcasted_iota(jnp.int32, (128, 128), 0)
    one = lax.broadcasted_iota(jnp.int32, (1, 128), 1)
    rows = [owner_ref[:, b * 128 : (b + 1) * 128].astype(F32) for b in range(nb)]
    cols = [column(r) for r in rows]
    dests = []
    for b in range(nb):
        rank = jnp.sum(jnp.where((cols[b] == rows[b]) & (sub < lane), 1.0, 0.0), axis=0, keepdims=True)
        for e in range(b):
            rank = rank + jnp.sum(jnp.where(cols[e] == rows[b], 1.0, 0.0), axis=0, keepdims=True)
        owner = rows[b].astype(jnp.int32)
        device = owner >> 1
        dest = (device & 1) * (CHIPS * 8) + (device >> 1) * 8 + (owner & 1) * 4 + rank.astype(jnp.int32)
        dests.append(jnp.where(one + b * 128 < LINES, dest, -1).astype(F32))
    dcols = [column(d) for d in dests]
    values = []
    for b in range(nb):
        j = sub + b * 128
        group = jnp.zeros_like(j)
        for g in range(1, G):
            group = group + jnp.where(j >= g * 120, 1, 0)
        place = j - group * 120 + turn * BV
        place = jnp.where(place >= 120, place - 120, place)
        values.append((group * 128 + place - EMPTY).astype(F32))
    out = []
    for d in range(8):
        want = (lane + d * 128).astype(F32)
        total = jnp.zeros((128, 128), F32)
        for b in range(nb):
            total = total + jnp.where(dcols[b] == want, values[b], 0.0)
        out.append(jnp.sum(total, axis=0, keepdims=True) + float(EMPTY))
    return jnp.concatenate(out, axis=0)


def first_kernel(turn_ref, x_ref, owner_ref, table_ref, out_ref):
    turn = turn_ref[0]
    codes = slot_codes(owner_ref, turn)
    for j in range(CHIPS):
        out_ref[pl.ds(j * 48 + 40, 8), :] = codes
    parts = []
    for g in range(G):
        for k in range(3):
            i = jnp.where(k >= turn, k - turn, k - turn + 3)
            u = g * 3 + i
            at = pl.multiple_of(jnp.minimum(u, BU - 1) * BV, 8)
            part = x_ref[pl.ds(at, BV), :]
            parts.append(part if g < G - 1 else jnp.where(u < BU, part, 0.0))
        parts.append(jnp.zeros((8, N), F32))
    hi, lo = split(jnp.concatenate(parts, axis=0))
    th, tl = table_ref[:, 0:N], table_ref[:, N : 2 * N]
    y = dot_nt(th, hi) + (dot_nt(th, lo) + dot_nt(tl, hi))
    zero = jnp.zeros((CHIPS, 128), F32)
    for q in range(Q):
        for g in range(G):
            out_ref[pl.ds(q * 8 + g, CHIPS, stride=48), :] = y[q * CHIPS : (q + 1) * CHIPS, g * 128 : (g + 1) * 128]
        out_ref[pl.ds(q * 8 + G, CHIPS, stride=48), :] = zero


def middle_kernel(
    core_ref, own_ref, oth_ref, kern_ref, swap_ref, t1_ref, a2_ref, s3_ref, d3_ref, t4_ref,
    out_ref, u_ref, l4_ref, even_ref, odd_ref, turn_ref, code_ref,
):
    core = core_ref[0]
    mine = core == 0
    lane = lax.broadcasted_iota(jnp.int32, (1, 128), 1)

    pieces = []
    for z in range(ZS):
        a = own_ref[:, z, 0:40, :].reshape(ROWS * 40, 128)
        b = oth_ref[:, z, 0:40, :].reshape(ROWS * 40, 128)
        pieces.append(jnp.where(mine, a, b))
        pieces.append(jnp.where(mine, b, a))
    for i in range(3):
        cols = []
        for v in range(3):
            part = [pieces[3 * v + (k - i) % 3] if 3 * v + (k - i) % 3 < 8 else None for k in range(3)]
            total = part[0] if part[0] is not None else part[1]
            for k in range(1, 3):
                if part[k] is not None and part[k] is not total:
                    total = jnp.where(lane >= k * BV, part[k], total)
            cols.append(total)
        u_ref[i] = dot(lhs_split(jnp.concatenate(cols, axis=1)), t1_ref[i]).reshape(ROWS, Q, 8, 384)

    ca, cb = swap_ref[0:1, :], swap_ref[1:2, :]

    def plane(q, carry):
        parts = [u_ref[i, :, pl.ds(q, 1), :, :].reshape(ROWS * 8, 384) for i in range(3)]
        value = dot(a2_ref[...], rhs_split(jnp.concatenate(parts, axis=0))) * kern_ref[q]
        swapped = []
        for v in range(3):
            at = slice(v * 128, (v + 1) * 128)
            part = value[:, at]
            swapped.append(pltpu.roll(part, 127, 1) * ca[:, at] + pltpu.roll(part, 1, 1) * cb[:, at])
        plain = rhs_split(value)
        fields = (
            dot(d3_ref[...], plain),
            dot(s3_ref[...], rhs_split(jnp.concatenate(swapped, axis=1))),
            dot(s3_ref[...], plain),
        )
        for f in range(3):
            for i in range(3):
                l4_ref[i, f * Q + q] = fields[f][i * 128 : (i + 1) * 128]
        return carry

    lax.fori_loop(0, Q, plane, 0)

    def sort_codes(r, carry):
        for zc in range(8):
            z, c = zc // 2, zc % 2
            blk = jnp.where(core == c, own_ref[r, z, 40:48, :], oth_ref[r, z, 40:48, :])
            code_ref[pl.ds(r * 32 + zc, 4, stride=8), :] = jnp.where(mine, blk[0:4], blk[4:8]).astype(jnp.int32)
        return carry

    lax.fori_loop(0, ROWS, sort_codes, 0)

    def lines_of(k, ref):
        at = pl.ds(pl.multiple_of(k * 16, 16), 16)
        ys = []
        for i in range(3):
            value = l4_ref[i, :, at, :].reshape(FQ * 16, 384)
            ys.append(dot(mix_split(value), t4_ref[i]).reshape(FQ, 16, 384))
            yield
        for zc in range(8):
            v, w = zc // 3, zc % 3
            total = None
            for k3 in range(3):
                part = ys[(k3 - w) % 3][:, :, v * 128 : (v + 1) * 128]
                total = part if total is None else jnp.where(lane >= k3 * BV, part, total)
            for rr in range(2):
                ref[rr, pl.ds(zc, FQ * 8, stride=8), :] = total[:, rr * 8 : rr * 8 + 8].reshape(FQ * 8, 128)
            if zc % 2:
                yield

    def pick(k, ref):
        for rr in range(2):
            for d in range(4):
                r = 2 * k + rr
                idx = code_ref[pl.ds(pl.multiple_of(r * 32 + d * 8, 8), 8), :]
                at, group = idx & 127, idx >> 7
                here = [group == g for g in range(G)]
                for pf in range(FQ):
                    acc = jnp.zeros((8, 128), F32)
                    for g in range(G):
                        part = ref[rr, (pf * 8 + g) * 8 : (pf * 8 + g) * 8 + 8, :]
                        acc = jnp.where(here[g], jnp.take_along_axis(part, at, axis=1), acc)
                    turn_ref[d, pl.ds(pl.multiple_of(pf * 128 + r * 8, 8), 8), :] = acc
                yield

    def together(*works):
        works = list(works)
        while works:
            works = [w for w in works if next(w, 0) is None]

    pairs = ROWS // 2
    together(lines_of(0, even_ref))

    def rows4(k, carry):
        together(lines_of(2 * k + 1, odd_ref), pick(2 * k, even_ref))
        together(lines_of(jnp.minimum(2 * k + 2, pairs - 1), even_ref), pick(2 * k + 1, odd_ref))
        return carry

    lax.fori_loop(0, pairs // 2, rows4, 0)

    def turned(pf, carry):
        for d in range(4):
            block = turn_ref[d, pl.ds(pf * 128, 128), :]
            out_ref[pl.ds(d * 128 * FQ + pf, 128, stride=FQ), :] = jnp.transpose(block)
        return carry

    lax.fori_loop(0, FQ, turned, 0)


def last_kernel(x_ref, s5_ref, d5_ref, out_ref):
    k = pl.program_id(0)

    def load(slot, f):
        parts = [x_ref[pl.ds(slot * FQ + f * Q + q, CHIPS, stride=8 * FQ), :] for q in range(Q)]
        return jnp.concatenate(parts, axis=0)

    for e in range(2):
        both = rhs_split(jnp.concatenate([load(2 * k + e, 0), load(2 * k + e, 1)], axis=1))
        y = dot(s5_ref[...], both)
        out_ref[e, 0] = y[:, 0:128]
        out_ref[e, 1] = y[:, 128:256]
    both = rhs_split(jnp.concatenate([load(2 * k, 2), load(2 * k + 1, 2)], axis=1))
    y = dot(d5_ref[...], both)
    out_ref[0, 2] = y[:, 0:128]
    out_ref[1, 2] = y[:, 128:256]


VM = pl.BlockSpec(memory_space=pltpu.VMEM)
SM = pl.BlockSpec(memory_space=pltpu.SMEM)


def params(mib):
    return pltpu.CompilerParams(vmem_limit_bytes=mib * 2**20)


def first_call(turn, x, owner, table):
    return pl.pallas_call(
        first_kernel,
        out_shape=jax.ShapeDtypeStruct((CHIPS * 48, 128), F32),
        in_specs=[SM] + [VM] * 3,
        out_specs=VM,
        compiler_params=params(32),
    )(turn, x, owner, table)


def middle_call(core, own, oth, kern, t):
    return pl.pallas_call(
        middle_kernel,
        out_shape=jax.ShapeDtypeStruct((CHIPS * 8 * FQ, 128), F32),
        in_specs=[SM] + [VM] * 9,
        out_specs=VM,
        scratch_shapes=[
            pltpu.VMEM((3, ROWS, Q, 8, 384), F32),
            pltpu.VMEM((3, FQ, 128, 384), F32),
            pltpu.VMEM((2, FQ * 64, 128), F32),
            pltpu.VMEM((2, FQ * 64, 128), F32),
            pltpu.VMEM((4, FQ * 128, 128), F32),
            pltpu.VMEM((ROWS * 32, 128), jnp.int32),
        ],
        compiler_params=params(40),
    )(core, own, oth, kern, t["swap"], t["t1"], t["a2"], t["s3"], t["d3"], t["t4"])


def last_call(x, s5, d5):
    return pl.pallas_call(
        last_kernel,
        grid=(4,),
        out_shape=jax.ShapeDtypeStruct((8, 3, N, 128), F32),
        in_specs=[VM] * 3,
        out_specs=pl.BlockSpec((2, 3, N, 128), lambda k: (k, 0, 0, 0)),
        compiler_params=params(32),
    )(x, s5, d5)


def filter_table(chip):
    def wave(p):
        return (p // 2).astype(F32) * STEP

    ka = wave(chip * Q + lax.iota(jnp.int32, Q))[:, None, None]
    kb = wave(lax.iota(jnp.int32, N))[None, :, None]
    kc = wave(lax.iota(jnp.int32, 384))[None, None, :]
    k2 = ka * ka + kb * kb + kc * kc
    off = (k2 <= 0.0) | (lax.iota(jnp.int32, 384)[None, None, :] >= N)
    safe = jnp.where(off, 1.0, k2)
    return jnp.where(off, 0.0, GAIN * safe ** (-0.75) / (1.0 + safe))


def local(noise, owners):
    t = make_tables()
    x = noise.transpose(1, 2, 0).reshape(LINES, N)
    owner = jnp.pad(owners.reshape(1, LINES), ((0, 0), (0, 896 - LINES)))
    core = lax.axis_index("core").astype(jnp.int32).reshape(1)
    turn = (lax.axis_index("z").astype(jnp.int32) * CORES + core) % 3
    sent = first_call(turn, x, owner, t["first"]).reshape(CHIPS, 48, 128)
    own = lax.all_to_all(sent, ("row", "z"), split_axis=0, concat_axis=0, tiled=True)
    oth = lax.ppermute(own, "core", [(0, 1), (1, 0)])
    chip = lax.axis_index("row") * ZS + lax.axis_index("z")
    shape = (ROWS, ZS, 48, 128)
    slots = middle_call(core, own.reshape(shape), oth.reshape(shape), filter_table(chip), t)
    got = lax.all_to_all(slots.reshape(CHIPS, 8 * FQ, 128), ("row", "z"), split_axis=0, concat_axis=0, tiled=True)
    out = last_call(got.reshape(CHIPS * 8 * FQ, 128), t["s5"], t["d5"])
    return out.reshape(2, 4, 3, N, 128).transpose(4, 0, 1, 2, 3)[None]


def solution(mesh):
    fine = Mesh(mesh.devices.reshape(ROWS, ZS, CORES), ("row", "z", "core"))
    every = ("row", "z", "core")
    in_specs = (P(None, "row", ("z", "core")), P(every, None, None))
    out_specs = P(every, None, None, None, None, None)
    return jax.shard_map(local, mesh=fine, in_specs=in_specs, out_specs=out_specs, check_vma=False)
```

time: 152 us -> 135 us (0.89)
  Pallas kernels: 50.7 us -> 32.8 us
  local copies, waits for them, and re-layouts: 4.25 us -> 8.21 us
  blocking collectives: 93.2 us -> 90.4 us
    pallas_call x2, Pallas kernels: 49 us -> 31.1 us  [the longest x1 26.9 us: middle_call(): pl.pallas_call(middle_kernel, out_shape=jax.ShapeDtypeStruct((CHIPS * 8 *...]
    unnamed x12 -> x20, local copies, waits for them, and re-layouts: 3.56 us -> 7.52 us
    all_to_all x1, blocking collectives: 57.6 us -> 54.9 us  [local(): lax.all_to_all(slots.reshape(CHIPS, 8 * FQ, 128), ('row', 'z'), split_axi...]
  transfers between devices with their start and end apart: 1 -> 1, of which waited for: 0 -> 1; matrix products, arithmetic and copies ran while one was open for 2% -> 1% of each run, Pallas kernels for 0% -> 0%
where the time goes in v2:
time: 135 us
  blocking collectives  90.4 us (67%)
  Pallas kernels  32.8 us (24%)
  local copies, waits for them, and re-layouts  8.21 us (6%)
  other arithmetic  1.93 us (1%)
  waiting for transfers between devices  1.46 us (1%)
    all_to_all x1, blocking collectives, local(): lax.all_to_all(slots.reshape(CHIPS, 8 * FQ, 128), ('row', 'z'), split_axi...  54.9 us
    all_to_all x1, blocking collectives, local(): lax.all_to_all(sent, ('row', 'z'), split_axis=0, concat_axis=0, tiled=True)  35.5 us
    pallas_call x1, Pallas kernels, middle_call(): pl.pallas_call(middle_kernel, out_shape=jax.ShapeDtypeStruct((CHIPS * 8 *...  26.9 us
    unnamed x20, local copies, waits for them, and re-layouts  7.52 us
    pallas_call x1, Pallas kernels, last_call(): pl.pallas_call(last_kernel, grid=(4,), out_shape=jax.ShapeDtypeStruct((8,...  4.17 us
  transfers between devices with their start and end apart: 1, of which 1 were waited for; matrix products, arithmetic and copies ran while one was open for 1% of the time, Pallas kernels for 0%

profile of v2, /device:TPU:0, one launch (start us, length us, event | category | flops | bytes accessed | tf_op | source)
XLA Modules:
  0.0 134.9 jit_solution(7801530222755130674)
XLA Ops:
  0.0 0.7 pad.4.owner_ref
  0.7 0.0 copy-start.2
  0.7 1.3 copy-done.2
  2.0 0.0 copy-start.8
  2.0 1.1 copy-done.8
  3.1 1.8 %shard_map.109 = f32[3072,128]{1,0:T(8,128)S(1)} custom-call(s32[1]{0:T(128)S(6)} %select_n.41.turn_ref, f32[800,320]{1,0:T(8,128)S(1)} %bitcast.20, s32[1,896]{1,0:T(1,128)S(1)} %pad.4.owner_ref, bf16[320,960]{1,0:T(8,128)(2,1)S(1)} %copy-done.8), custom_call_target="tpu_custom_call" | custom-call | tf_op jit(solution)/shard_map/pallas_call | solution.py:344
  4.8 0.0 copy-start.9
  4.9 35.5 %all_to_all.10 = f32[64,48,128]{2,1,0:T(8,128)S(1)} all-to-all(f32[64,48,128]{2,1,0:T(8,128)S(1)} %bitcast.18), channel_id=1, replica_groups=mesh['row'=16,'z'=4,'core'=2] {'row','z'}, dimensions={0} | all-to-all | bytes 3145728 | tf_op jit(solution)/shard_map/all_to_all | solution.py:402
  40.4 0.0 collective-permute-start
  40.4 0.0 copy-start.1
  40.4 0.1 broadcast_add_fusion
  40.5 1.8 %fusion.4.kern_ref = f32[5,320,384]{2,1,0:T(8,128)S(1)} fusion(f32[384]{0:T(512)S(1)} %fusion.11, f32[5,320]{1,0:T(8,128)S(1)} %broadcast_add_fusion, pred[384]{0:T(512)(128)(4,1)S(1)} %iota_compare_fusion), kind=kLoop, calls=%fused_computation.6 | loop fusion | flops 4915200 | bytes 2465920 | tf_op jit(solution)/shard_map/jit(_where)/select_n | solution.py:392
  42.3 1.5 %collective-permute-done = f32[64,48,128]{2,1,0:T(8,128)S(1)} collective-permute-done((f32[64,48,128]{2,1,0:T(8,128)S(1)}, f32[64,48,128]{2,1,0:T(8,128)S(1)}, u32[]{:S(2)}, u32[]{:S(2)}) %collective-permute-start) | collective-permute-done | bytes 1572896 | tf_op jit(solution)/shard_map/ppermute | solution.py:403
  43.8 0.0 copy-done.9
  43.8 0.0 copy-done.1
  43.8 0.0 copy-start
  43.8 1.7 %copy-done = bf16[3,1152,384]{2,1,0:T(8,128)(2,1)S(1)} copy-done((bf16[3,1152,384]{2,1,0:T(8,128)(2,1)S(1)}, bf16[3,1152,384]{2,1,0:T(8,128)(2,1)}, u32[]{:S(2)}) %copy-start) | copy-done | bytes 2654232
  45.6 0.0 copy-start.3
  45.6 1.1 copy-done.3
  46.7 0.0 copy-start.4
  46.7 1.1 copy-done.4
  47.8 0.0 copy-start.5
  47.8 1.1 copy-done.5
  48.9 26.9 %shard_map.110 = f32[7680,128]{1,0:T(8,128)} custom-call(s32[1]{0:T(128)} %bitcast.core_ref, f32[16,4,48,128]{3,2,1,0:T(8,128)S(1)} %bitcast.17, f32[16,4,48,128]{3,2,1,0:T(8,128)S(1)} %bitcast.19, f32[5,320,384]{2,1,0:T(8,128)S(1)} %fusion.4.kern_ref, f32[8,384]{1,0:T(8,128)S(1)} %copy-done.9, bf16[3,1152,384]{2,1,0:T(8,128)(2,1)S(1)} %copy-done, ...), custom_call_target="tpu_custom_call" | custom-call | tf_op jit(solution)/shard_map/pallas_call | solution.py:354
  75.8 0.0 copy-start.6
  75.8 0.0 copy-start.7
  75.8 54.9 %all_to_all.11 = f32[64,120,128]{2,1,0:T(8,128)S(1)} all-to-all(f32[64,120,128]{2,1,0:T(8,128)} %bitcast.21), channel_id=1, replica_groups=mesh['row'=16,'z'=4,'core'=2] {'row','z'}, dimensions={0} | all-to-all | bytes 7864320 | tf_op jit(solution)/shard_map/all_to_all | solution.py:407
  130.7 0.0 copy-done.6
  130.8 0.0 copy-done.7
  130.8 4.2 %shard_map.111 = f32[8,3,320,128]{3,2,1,0:T(8,128)} custom-call(f32[7680,128]{1,0:T(8,128)S(1)} %bitcast.16, bf16[320,960]{1,0:T(8,128)(2,1)S(1)} %copy-done.7, bf16[320,960]{1,0:T(8,128)(2,1)S(1)} %copy-done.6), custom_call_target="tpu_custom_call" | custom-call | tf_op jit(solution)/shard_map/pallas_call | solution.py:372
  (4 shorter events, 0.0 us)
Async XLA Ops:
  0.7 1.3 copy-start.2
  2.0 1.1 copy-start.8
  4.8 39.0 %copy-start.9 = (f32[8,384]{1,0:T(8,128)S(1)}, f32[8,384]{1,0:T(8,128)}, u32[]{:S(2)}) copy-start(f32[8,384]{1,0:T(8,128)} %constant.104.clone.swap_ref) | copy-start | bytes 36868
  40.4 3.4 %collective-permute-start = (f32[64,48,128]{2,1,0:T(8,128)S(1)}, f32[64,48,128]{2,1,0:T(8,128)S(1)}, u32[]{:S(2)}, u32[]{:S(2)}) collective-permute-start(f32[64,48,128]{2,1,0:T(8,128)S(1)} %all_to_all.10), channel_id=1, source_target_pairs={{0,1},{1,0},{2,3},{3,2},{4,5},{5,4},{6,7},{7,6},{8,9},{9,8},{10,11... | collective-permute-start | bytes 4718600 | tf_op jit(solution)/shard_map/ppermute | solution.py:403
  40.4 3.4 %copy-start.1 = (bf16[3,1024,384]{2,1,0:T(8,128)(2,1)S(1)}, bf16[3,1024,384]{2,1,0:T(8,128)(2,1)}, u32[]{:S(2)}) copy-start(bf16[3,1024,384]{2,1,0:T(8,128)(2,1)} %constant.109.clone.t4_ref) | copy-start | bytes 7077892
  43.8 1.8 %copy-start = (bf16[3,1152,384]{2,1,0:T(8,128)(2,1)S(1)}, bf16[3,1152,384]{2,1,0:T(8,128)(2,1)}, u32[]{:S(2)}) copy-start(bf16[3,1152,384]{2,1,0:T(8,128)(2,1)} %constant.105.clone.t1_ref) | copy-start | bytes 7962628
  45.6 1.1 copy-start.3
  46.7 1.1 copy-start.4
  47.8 1.1 copy-start.5
  75.8 54.9 %copy-start.6 = (bf16[320,960]{1,0:T(8,128)(2,1)S(1)}, bf16[320,960]{1,0:T(8,128)(2,1)}, u32[]{:S(2)}) copy-start(bf16[320,960]{1,0:T(8,128)(2,1)} %constant.111.clone.d5_ref) | copy-start | bytes 1843204
  75.8 54.9 %copy-start.7 = (bf16[320,960]{1,0:T(8,128)(2,1)S(1)}, bf16[320,960]{1,0:T(8,128)(2,1)}, u32[]{:S(2)}) copy-start(bf16[320,960]{1,0:T(8,128)(2,1)} %constant.110.clone.s5_ref) | copy-start | bytes 1843204

commit v3 on v2

--- a/solution.py
+++ b/solution.py
@@ -90,13 +90,17 @@
     even = np.arange(384) % 2 == 0
     swap = np.zeros((8, 384), np.float32)
     swap[0], swap[1] = np.where(even, kw, 0.0), np.where(even, 0.0, -kw)
+    def wide(table):
+        table = np.pad(lhs_table(table), ((0, 0), (0, 1152)))
+        return [table[:, k * 384 : (k + 1) * 384] for k in range(3)]
+
+    blocks = [rhs_table(t) for t in t1]
+    for table in (a2.reshape(N, 384), d3.reshape(384, N), s3.reshape(384, N)):
+        blocks += wide(table)
+    blocks += [mix_table(t) for t in t4]
     return dict(
         first=lhs_table(first),
-        t1=np.stack([rhs_table(t) for t in t1]),
-        a2=lhs_table(a2.reshape(N, 384)),
-        s3=lhs_table(s3.reshape(384, N)),
-        d3=lhs_table(d3.reshape(384, N)),
-        t4=np.stack([mix_table(t) for t in t4]),
+        middle=np.concatenate(blocks, axis=0),
         s5=lhs_table(s5),
         d5=lhs_table(d5),
         swap=swap,
@@ -145,7 +149,8 @@
     lane = lax.broadcasted_iota(jnp.int32, (128, 128), 1)
     sub = lax.broadcasted_iota(jnp.int32, (128, 128), 0)
     one = lax.broadcasted_iota(jnp.int32, (1, 128), 1)
-    rows = [owner_ref[:, b * 128 : (b + 1) * 128].astype(F32) for b in range(nb)]
+    last = jnp.concatenate([owner_ref[:, 768:LINES], jnp.zeros((1, 896 - LINES), jnp.int32)], axis=1)
+    rows = [(owner_ref[:, b * 128 : (b + 1) * 128] if b < nb - 1 else last).astype(F32) for b in range(nb)]
     cols = [column(r) for r in rows]
     dests = []
     for b in range(nb):
@@ -176,11 +181,19 @@
     return jnp.concatenate(out, axis=0)
 
 
-def first_kernel(turn_ref, x_ref, owner_ref, table_ref, out_ref):
+def first_kernel(turn_ref, x_hbm, owner_ref, table_hbm, out_ref, x_ref, table_ref, sems):
+    copies = [
+        pltpu.make_async_copy(x_hbm, x_ref, sems.at[0]),
+        pltpu.make_async_copy(table_hbm, table_ref, sems.at[1]),
+    ]
+    for copy in copies:
+        copy.start()
     turn = turn_ref[0]
     codes = slot_codes(owner_ref, turn)
     for j in range(CHIPS):
         out_ref[pl.ds(j * 48 + 40, 8), :] = codes
+    for copy in copies:
+        copy.wait()
     parts = []
     for g in range(G):
         for k in range(3):
@@ -201,9 +214,20 @@
 
 
 def middle_kernel(
-    core_ref, own_ref, oth_ref, kern_ref, swap_ref, t1_ref, a2_ref, s3_ref, d3_ref, t4_ref,
-    out_ref, u_ref, l4_ref, even_ref, odd_ref, turn_ref, code_ref,
+    core_ref, own_ref, oth_ref, kern_ref, swap_ref, table_hbm,
+    out_ref, u_ref, l4_ref, even_ref, odd_ref, turn_ref, code_ref, t1_ref, a2_ref, d3_ref, s3_ref, t4_ref, sems,
 ):
+    fetches = []
+    row = 0
+    targets = [t1_ref.at[i] for i in range(3)]
+    for ref in (a2_ref, d3_ref, s3_ref):
+        targets += [ref.at[:, k * 384 : (k + 1) * 384] for k in range(3)]
+    targets += [t4_ref.at[i] for i in range(3)]
+    for k, target in enumerate(targets):
+        rows = target.shape[0]
+        fetches.append(pltpu.make_async_copy(table_hbm.at[row : row + rows], target, sems.at[k]))
+        fetches[-1].start()
+        row += rows
     core = core_ref[0]
     mine = core == 0
     lane = lax.broadcasted_iota(jnp.int32, (1, 128), 1)
@@ -223,6 +247,7 @@
                 if part[k] is not None and part[k] is not total:
                     total = jnp.where(lane >= k * BV, part[k], total)
             cols.append(total)
+        fetches[i].wait()
         u_ref[i] = dot(lhs_split(jnp.concatenate(cols, axis=1)), t1_ref[i]).reshape(ROWS, Q, 8, 384)
 
     ca, cb = swap_ref[0:1, :], swap_ref[1:2, :]
@@ -237,16 +262,18 @@
             swapped.append(pltpu.roll(part, 127, 1) * ca[:, at] + pltpu.roll(part, 1, 1) * cb[:, at])
         plain = rhs_split(value)
         fields = (
-            dot(d3_ref[...], plain),
-            dot(s3_ref[...], rhs_split(jnp.concatenate(swapped, axis=1))),
-            dot(s3_ref[...], plain),
+            dot(d3_ref[:, : 3 * N], plain),
+            dot(s3_ref[:, : 3 * N], rhs_split(jnp.concatenate(swapped, axis=1))),
+            dot(s3_ref[:, : 3 * N], plain),
         )
         for f in range(3):
             for i in range(3):
                 l4_ref[i, f * Q + q] = fields[f][i * 128 : (i + 1) * 128]
         return carry
 
-    lax.fori_loop(0, Q, plane, 0)
+    for fetch in fetches[3:12]:
+        fetch.wait()
+    lax.fori_loop(0, Q, plane, 0, unroll=True)
 
     def sort_codes(r, carry):
         for zc in range(8):
@@ -296,6 +323,8 @@
             works = [w for w in works if next(w, 0) is None]
 
     pairs = ROWS // 2
+    for fetch in fetches[12:]:
+        fetch.wait()
     together(lines_of(0, even_ref))
 
     def rows4(k, carry):
@@ -307,18 +336,20 @@
 
     def turned(pf, carry):
         for d in range(4):
-            block = turn_ref[d, pl.ds(pf * 128, 128), :]
-            out_ref[pl.ds(d * 128 * FQ + pf, 128, stride=FQ), :] = jnp.transpose(block)
+            block = jnp.transpose(turn_ref[d, pl.ds(pl.multiple_of(pf * 128, 128), 128), :])
+            for c in range(16):
+                at = pl.multiple_of((d * 16 + c) * 8 * FQ + pf * 8, 8)
+                out_ref[pl.ds(at, 8), :] = block[c * 8 : c * 8 + 8]
         return carry
 
-    lax.fori_loop(0, FQ, turned, 0)
+    lax.fori_loop(0, FQ, turned, 0, unroll=5)
 
 
 def last_kernel(x_ref, s5_ref, d5_ref, out_ref):
     k = pl.program_id(0)
 
     def load(slot, f):
-        parts = [x_ref[pl.ds(slot * FQ + f * Q + q, CHIPS, stride=8 * FQ), :] for q in range(Q)]
+        parts = [x_ref[pl.ds((f * Q + q) * 8 + slot, CHIPS, stride=8 * FQ), :] for q in range(Q)]
         return jnp.concatenate(parts, axis=0)
 
     for e in range(2):
@@ -334,6 +365,7 @@
 
 VM = pl.BlockSpec(memory_space=pltpu.VMEM)
 SM = pl.BlockSpec(memory_space=pltpu.SMEM)
+HB = pl.BlockSpec(memory_space=pltpu.HBM)
 
 
 def params(mib):
@@ -344,17 +376,23 @@
     return pl.pallas_call(
         first_kernel,
         out_shape=jax.ShapeDtypeStruct((CHIPS * 48, 128), F32),
-        in_specs=[SM] + [VM] * 3,
+        in_specs=[SM, HB, VM, HB],
         out_specs=VM,
-        compiler_params=params(32),
+        scratch_shapes=[
+            pltpu.VMEM(x.shape, F32),
+            pltpu.VMEM(table.shape, BF16),
+            pltpu.SemaphoreType.DMA((2,)),
+        ],
+        compiler_params=params(60),
     )(turn, x, owner, table)
 
 
 def middle_call(core, own, oth, kern, t):
+    shapes = ((3, 1152, 384), (N, 1152), (384, 1152), (384, 1152), (3, 1024, 384))
     return pl.pallas_call(
         middle_kernel,
         out_shape=jax.ShapeDtypeStruct((CHIPS * 8 * FQ, 128), F32),
-        in_specs=[SM] + [VM] * 9,
+        in_specs=[SM] + [VM] * 4 + [HB],
         out_specs=VM,
         scratch_shapes=[
             pltpu.VMEM((3, ROWS, Q, 8, 384), F32),
@@ -363,9 +401,11 @@
             pltpu.VMEM((2, FQ * 64, 128), F32),
             pltpu.VMEM((4, FQ * 128, 128), F32),
             pltpu.VMEM((ROWS * 32, 128), jnp.int32),
-        ],
-        compiler_params=params(40),
-    )(core, own, oth, kern, t["swap"], t["t1"], t["a2"], t["s3"], t["d3"], t["t4"])
+        ]
+        + [pltpu.VMEM(shape, BF16) for shape in shapes]
+        + [pltpu.SemaphoreType.DMA((15,))],
+        compiler_params=params(42),
+    )(core, own, oth, kern, t["swap"], t["middle"])
 
 
 def last_call(x, s5, d5):
@@ -395,7 +435,7 @@
 def local(noise, owners):
     t = make_tables()
     x = noise.transpose(1, 2, 0).reshape(LINES, N)
-    owner = jnp.pad(owners.reshape(1, LINES), ((0, 0), (0, 896 - LINES)))
+    owner = owners.reshape(1, LINES)
     core = lax.axis_index("core").astype(jnp.int32).reshape(1)
     turn = (lax.axis_index("z").astype(jnp.int32) * CORES + core) % 3
     sent = first_call(turn, x, owner, t["first"]).reshape(CHIPS, 48, 128)

time: 135 us -> 128 us (0.948)
  local copies, waits for them, and re-layouts: 8.21 us -> 0.02 us
  Pallas kernels: 32.8 us -> 34.5 us
    unnamed x20 -> x6, local copies, waits for them, and re-layouts: 7.52 us -> 0.02 us
    pallas_call x1, Pallas kernels: 1.77 us -> 4.74 us  [first_call(): pl.pallas_call(first_kernel, out_shape=jax.ShapeDtypeStruct((CHIPS * 48,...]
    pallas_call x1, Pallas kernels: 26.9 us -> 25.5 us  [middle_call(): pl.pallas_call(middle_kernel, out_shape=jax.ShapeDtypeStruct((CHIPS * 8 *...]
  transfers between devices with their start and end apart: 1 -> 1, of which waited for: 1 -> 1; matrix products, arithmetic and copies ran while one was open for 1% -> 2% of each run, Pallas kernels for 0% -> 0%
where the time goes in v3:
time: 128 us
  blocking collectives  90.1 us (70%)
  Pallas kernels  34.5 us (27%)
  other arithmetic  1.93 us (2%)
  waiting for transfers between devices  1.46 us (1%)
    all_to_all x1, blocking collectives, local(): lax.all_to_all(slots.reshape(CHIPS, 8 * FQ, 128), ('row', 'z'), split_axi...  54.3 us
    all_to_all x1, blocking collectives, local(): lax.all_to_all(sent, ('row', 'z'), split_axis=0, concat_axis=0, tiled=True)  35.8 us
    pallas_call x1, Pallas kernels, middle_call(): pl.pallas_call(middle_kernel, out_shape=jax.ShapeDtypeStruct((CHIPS * 8 *...  25.5 us
    pallas_call x1, Pallas kernels, first_call(): pl.pallas_call(first_kernel, out_shape=jax.ShapeDtypeStruct((CHIPS * 48,...  4.74 us
    pallas_call x1, Pallas kernels, last_call(): pl.pallas_call(last_kernel, grid=(4,), out_shape=jax.ShapeDtypeStruct((8,...  4.32 us
  transfers between devices with their start and end apart: 1, of which 1 were waited for; matrix products, arithmetic and copies ran while one was open for 2% of the time, Pallas kernels for 0%

profile of v3, /device:TPU:0, one launch (start us, length us, event | category | flops | bytes accessed | tf_op | source)
XLA Modules:
  0.0 128.1 jit_solution(18151614225420940846)
XLA Ops:
  0.0 4.7 %shard_map.73 = f32[3072,128]{1,0:T(8,128)} custom-call(s32[1]{0:T(128)S(6)} %select_n.41.turn_ref, f32[800,320]{1,0:T(8,128)} %bitcast.21, s32[1,800]{1,0:T(1,128)} %bitcast.22, bf16[320,960]{1,0:T(8,128)(2,1)} %constant.94.clone.table_hbm), custom_call_target="tpu_custom_call" | custom-call | tf_op jit(solution)/shard_map/pallas_call | solution.py:376
  4.8 0.0 copy-start.2
  4.8 35.8 %all_to_all.10 = f32[64,48,128]{2,1,0:T(8,128)S(1)} all-to-all(f32[64,48,128]{2,1,0:T(8,128)} %bitcast.20), channel_id=1, replica_groups=mesh['row'=16,'z'=4,'core'=2] {'row','z'}, dimensions={0} | all-to-all | bytes 3145728 | tf_op jit(solution)/shard_map/all_to_all | solution.py:442
  40.5 0.0 collective-permute-start
  40.6 0.1 broadcast_add_fusion
  40.6 1.8 %fusion.4.kern_ref = f32[5,320,384]{2,1,0:T(8,128)S(1)} fusion(f32[384]{0:T(512)S(1)} %fusion.11, f32[5,320]{1,0:T(8,128)S(1)} %broadcast_add_fusion, pred[384]{0:T(512)(128)(4,1)S(1)} %iota_compare_fusion), kind=kLoop, calls=%fused_computation.6 | loop fusion | flops 4915200 | bytes 2465920 | tf_op jit(solution)/shard_map/jit(_where)/select_n | solution.py:432
  42.5 1.5 %collective-permute-done = f32[64,48,128]{2,1,0:T(8,128)S(1)} collective-permute-done((f32[64,48,128]{2,1,0:T(8,128)S(1)}, f32[64,48,128]{2,1,0:T(8,128)S(1)}, u32[]{:S(2)}, u32[]{:S(2)}) %collective-permute-start) | collective-permute-done | bytes 1572896 | tf_op jit(solution)/shard_map/ppermute | solution.py:443
  43.9 0.0 copy-done.2
  43.9 25.5 %shard_map.74 = f32[7680,128]{1,0:T(8,128)S(1)} custom-call(s32[1]{0:T(128)} %bitcast.core_ref, f32[16,4,48,128]{3,2,1,0:T(8,128)S(1)} %bitcast.18, f32[16,4,48,128]{3,2,1,0:T(8,128)S(1)} %bitcast.19, f32[5,320,384]{2,1,0:T(8,128)S(1)} %fusion.4.kern_ref, f32[8,384]{1,0:T(8,128)S(1)} %copy-done.2, bf16[9792,384]{1,0:T(8,128)(2,1)} %constant.96.clone.table_hbm), custom_call_target="tpu_custom_call" | custom-call | tf_op jit(solution)/shard_map/pallas_call | solution.py:392
  69.4 0.0 copy-start
  69.4 0.0 copy-start.1
  69.4 54.3 %all_to_all.11 = f32[64,120,128]{2,1,0:T(8,128)S(1)} all-to-all(f32[64,120,128]{2,1,0:T(8,128)S(1)} %bitcast.16), channel_id=1, replica_groups=mesh['row'=16,'z'=4,'core'=2] {'row','z'}, dimensions={0} | all-to-all | bytes 7864320 | tf_op jit(solution)/shard_map/all_to_all | solution.py:447
  123.8 0.0 copy-done
  123.8 0.0 copy-done.1
  123.8 4.3 %shard_map.75 = f32[8,3,320,128]{3,2,1,0:T(8,128)} custom-call(f32[7680,128]{1,0:T(8,128)S(1)} %bitcast.17, bf16[320,960]{1,0:T(8,128)(2,1)S(1)} %copy-done.1, bf16[320,960]{1,0:T(8,128)(2,1)S(1)} %copy-done), custom_call_target="tpu_custom_call" | custom-call | tf_op jit(solution)/shard_map/pallas_call | solution.py:412
  (4 shorter events, 0.0 us)
Async XLA Ops:
  4.8 39.2 %copy-start.2 = (f32[8,384]{1,0:T(8,128)S(1)}, f32[8,384]{1,0:T(8,128)}, u32[]{:S(2)}) copy-start(f32[8,384]{1,0:T(8,128)} %constant.95.clone.swap_ref) | copy-start | bytes 36868
  40.5 3.4 %collective-permute-start = (f32[64,48,128]{2,1,0:T(8,128)S(1)}, f32[64,48,128]{2,1,0:T(8,128)S(1)}, u32[]{:S(2)}, u32[]{:S(2)}) collective-permute-start(f32[64,48,128]{2,1,0:T(8,128)S(1)} %all_to_all.10), channel_id=1, source_target_pairs={{0,1},{1,0},{2,3},{3,2},{4,5},{5,4},{6,7},{7,6},{8,9},{9,8},{10,11... | collective-permute-start | bytes 4718600 | tf_op jit(solution)/shard_map/ppermute | solution.py:443
  69.4 54.3 %copy-start = (bf16[320,960]{1,0:T(8,128)(2,1)S(1)}, bf16[320,960]{1,0:T(8,128)(2,1)}, u32[]{:S(2)}) copy-start(bf16[320,960]{1,0:T(8,128)(2,1)} %constant.98.clone.d5_ref) | copy-start | bytes 1843204
  69.4 54.3 %copy-start.1 = (bf16[320,960]{1,0:T(8,128)(2,1)S(1)}, bf16[320,960]{1,0:T(8,128)(2,1)}, u32[]{:S(2)}) copy-start(bf16[320,960]{1,0:T(8,128)(2,1)} %constant.97.clone.s5_ref) | copy-start | bytes 1843204

commit v4 on v3

--- a/solution.py
+++ b/solution.py
@@ -18,6 +18,7 @@
 Q = 5
 CH = 48
 FQ = 3 * Q
+RR = 2
 G = 7
 LINES = BU * BV
 EMPTY = G * 128
@@ -252,28 +253,34 @@
 
     ca, cb = swap_ref[0:1, :], swap_ref[1:2, :]
 
-    def plane(q, carry):
-        parts = [u_ref[i, :, pl.ds(q, 1), :, :].reshape(ROWS * 8, 384) for i in range(3)]
-        value = dot(a2_ref[...], rhs_split(jnp.concatenate(parts, axis=0))) * kern_ref[q]
-        swapped = []
-        for v in range(3):
-            at = slice(v * 128, (v + 1) * 128)
-            part = value[:, at]
-            swapped.append(pltpu.roll(part, 127, 1) * ca[:, at] + pltpu.roll(part, 1, 1) * cb[:, at])
-        plain = rhs_split(value)
-        fields = (
-            dot(d3_ref[:, : 3 * N], plain),
-            dot(s3_ref[:, : 3 * N], rhs_split(jnp.concatenate(swapped, axis=1))),
-            dot(s3_ref[:, : 3 * N], plain),
-        )
-        for f in range(3):
-            for i in range(3):
-                l4_ref[i, f * Q + q] = fields[f][i * 128 : (i + 1) * 128]
-        return carry
+    def keep(f, q, y):
+        for i in range(3):
+            l4_ref[i, f * Q + q] = y[i * 128 : (i + 1) * 128]
 
     for fetch in fetches[3:12]:
         fetch.wait()
-    lax.fori_loop(0, Q, plane, 0, unroll=True)
+    for pair in ((0, 1), (2, 3), (4,)):
+        rhs = []
+        for q in pair:
+            parts = [u_ref[i, :, q, :, :].reshape(ROWS * 8, 384) for i in range(3)]
+            rhs.append(rhs_split(jnp.concatenate(parts, axis=0)))
+        analysed = dot(a2_ref[...], jnp.concatenate(rhs, axis=1))
+        plains = []
+        for k, q in enumerate(pair):
+            value = analysed[:, k * 384 : (k + 1) * 384] * kern_ref[q]
+            swapped = []
+            for v in range(3):
+                at = slice(v * 128, (v + 1) * 128)
+                part = value[:, at]
+                swapped.append(pltpu.roll(part, 127, 1) * ca[:, at] + pltpu.roll(part, 1, 1) * cb[:, at])
+            plains.append(rhs_split(value))
+            turned_rhs = rhs_split(jnp.concatenate(swapped, axis=1))
+            y = dot(s3_ref[:, : 3 * N], jnp.concatenate([turned_rhs, plains[-1]], axis=1))
+            keep(1, q, y[:, :384])
+            keep(2, q, y[:, 384:])
+        y = dot(d3_ref[:, : 3 * N], jnp.concatenate(plains, axis=1))
+        for k, q in enumerate(pair):
+            keep(0, q, y[:, k * 384 : (k + 1) * 384])
 
     def sort_codes(r, carry):
         for zc in range(8):
@@ -285,11 +292,11 @@
     lax.fori_loop(0, ROWS, sort_codes, 0)
 
     def lines_of(k, ref):
-        at = pl.ds(pl.multiple_of(k * 16, 16), 16)
+        at = pl.ds(pl.multiple_of(k * RR * 8, RR * 8), RR * 8)
         ys = []
         for i in range(3):
-            value = l4_ref[i, :, at, :].reshape(FQ * 16, 384)
-            ys.append(dot(mix_split(value), t4_ref[i]).reshape(FQ, 16, 384))
+            value = l4_ref[i, :, at, :].reshape(FQ * RR * 8, 384)
+            ys.append(dot(mix_split(value), t4_ref[i]).reshape(FQ, RR * 8, 384))
             yield
         for zc in range(8):
             v, w = zc // 3, zc % 3
@@ -297,15 +304,15 @@
             for k3 in range(3):
                 part = ys[(k3 - w) % 3][:, :, v * 128 : (v + 1) * 128]
                 total = part if total is None else jnp.where(lane >= k3 * BV, part, total)
-            for rr in range(2):
+            for rr in range(RR):
                 ref[rr, pl.ds(zc, FQ * 8, stride=8), :] = total[:, rr * 8 : rr * 8 + 8].reshape(FQ * 8, 128)
             if zc % 2:
                 yield
 
     def pick(k, ref):
-        for rr in range(2):
+        for rr in range(RR):
             for d in range(4):
-                r = 2 * k + rr
+                r = RR * k + rr
                 idx = code_ref[pl.ds(pl.multiple_of(r * 32 + d * 8, 8), 8), :]
                 at, group = idx & 127, idx >> 7
                 here = [group == g for g in range(G)]
@@ -322,17 +329,19 @@
         while works:
             works = [w for w in works if next(w, 0) is None]
 
-    pairs = ROWS // 2
+    steps = ROWS // RR
     for fetch in fetches[12:]:
         fetch.wait()
     together(lines_of(0, even_ref))
 
-    def rows4(k, carry):
+    def two(k, carry):
         together(lines_of(2 * k + 1, odd_ref), pick(2 * k, even_ref))
-        together(lines_of(jnp.minimum(2 * k + 2, pairs - 1), even_ref), pick(2 * k + 1, odd_ref))
+        together(lines_of(2 * k + 2, even_ref), pick(2 * k + 1, odd_ref))
         return carry
 
-    lax.fori_loop(0, pairs // 2, rows4, 0)
+    lax.fori_loop(0, steps // 2 - 1, two, 0)
+    together(lines_of(steps - 1, odd_ref), pick(steps - 2, even_ref))
+    together(pick(steps - 1, odd_ref))
 
     def turned(pf, carry):
         for d in range(4):
@@ -397,8 +406,8 @@
         scratch_shapes=[
             pltpu.VMEM((3, ROWS, Q, 8, 384), F32),
             pltpu.VMEM((3, FQ, 128, 384), F32),
-            pltpu.VMEM((2, FQ * 64, 128), F32),
-            pltpu.VMEM((2, FQ * 64, 128), F32),
+            pltpu.VMEM((RR, FQ * 64, 128), F32),
+            pltpu.VMEM((RR, FQ * 64, 128), F32),
             pltpu.VMEM((4, FQ * 128, 128), F32),
             pltpu.VMEM((ROWS * 32, 128), jnp.int32),
         ]

time: 128 us -> 126 us (0.984)
  Pallas kernels: 34.5 us -> 32.5 us
    pallas_call x1, Pallas kernels: 25.5 us -> 23.4 us  [middle_call(): pl.pallas_call(middle_kernel, out_shape=jax.ShapeDtypeStruct((CHIPS * 8 *...]
where the time goes in v4:
time: 126 us
  blocking collectives  90.1 us (72%)
  Pallas kernels  32.5 us (26%)
  other arithmetic  1.93 us (2%)
  waiting for transfers between devices  1.46 us (1%)
    all_to_all x1, blocking collectives, local(): lax.all_to_all(slots.reshape(CHIPS, 8 * FQ, 128), ('row', 'z'), split_axi...  54.3 us
    all_to_all x1, blocking collectives, local(): lax.all_to_all(sent, ('row', 'z'), split_axis=0, concat_axis=0, tiled=True)  35.8 us
    pallas_call x1, Pallas kernels, middle_call(): pl.pallas_call(middle_kernel, out_shape=jax.ShapeDtypeStruct((CHIPS * 8 *...  23.4 us
    pallas_call x1, Pallas kernels, first_call(): pl.pallas_call(first_kernel, out_shape=jax.ShapeDtypeStruct((CHIPS * 48,...  4.74 us
    pallas_call x1, Pallas kernels, last_call(): pl.pallas_call(last_kernel, grid=(4,), out_shape=jax.ShapeDtypeStruct((8,...  4.32 us
  transfers between devices with their start and end apart: 1, of which 1 were waited for; matrix products, arithmetic and copies ran while one was open for 2% of the time, Pallas kernels for 0%

profile of v4, /device:TPU:0, one launch (start us, length us, event | category | flops | bytes accessed | tf_op | source)
XLA Modules:
  0.0 126.0 jit_solution(6720911080462117312)
XLA Ops:
  0.0 4.7 %shard_map.73 = f32[3072,128]{1,0:T(8,128)} custom-call(s32[1]{0:T(128)S(6)} %select_n.41.turn_ref, f32[800,320]{1,0:T(8,128)} %bitcast.21, s32[1,800]{1,0:T(1,128)} %bitcast.22, bf16[320,960]{1,0:T(8,128)(2,1)} %constant.94.clone.table_hbm), custom_call_target="tpu_custom_call" | custom-call | tf_op jit(solution)/shard_map/pallas_call | solution.py:385
  4.8 0.0 copy-start.2
  4.8 35.8 %all_to_all.10 = f32[64,48,128]{2,1,0:T(8,128)S(1)} all-to-all(f32[64,48,128]{2,1,0:T(8,128)} %bitcast.20), channel_id=1, replica_groups=mesh['row'=16,'z'=4,'core'=2] {'row','z'}, dimensions={0} | all-to-all | bytes 3145728 | tf_op jit(solution)/shard_map/all_to_all | solution.py:451
  40.5 0.0 collective-permute-start
  40.6 0.1 broadcast_add_fusion
  40.6 1.8 %fusion.4.kern_ref = f32[5,320,384]{2,1,0:T(8,128)S(1)} fusion(f32[384]{0:T(512)S(1)} %fusion.11, f32[5,320]{1,0:T(8,128)S(1)} %broadcast_add_fusion, pred[384]{0:T(512)(128)(4,1)S(1)} %iota_compare_fusion), kind=kLoop, calls=%fused_computation.6 | loop fusion | flops 4915200 | bytes 2465920 | tf_op jit(solution)/shard_map/jit(_where)/select_n | solution.py:441
  42.5 1.5 %collective-permute-done = f32[64,48,128]{2,1,0:T(8,128)S(1)} collective-permute-done((f32[64,48,128]{2,1,0:T(8,128)S(1)}, f32[64,48,128]{2,1,0:T(8,128)S(1)}, u32[]{:S(2)}, u32[]{:S(2)}) %collective-permute-start) | collective-permute-done | bytes 1572896 | tf_op jit(solution)/shard_map/ppermute | solution.py:452
  43.9 0.0 copy-done.2
  43.9 23.4 %shard_map.74 = f32[7680,128]{1,0:T(8,128)S(1)} custom-call(s32[1]{0:T(128)} %bitcast.core_ref, f32[16,4,48,128]{3,2,1,0:T(8,128)S(1)} %bitcast.18, f32[16,4,48,128]{3,2,1,0:T(8,128)S(1)} %bitcast.19, f32[5,320,384]{2,1,0:T(8,128)S(1)} %fusion.4.kern_ref, f32[8,384]{1,0:T(8,128)S(1)} %copy-done.2, bf16[9792,384]{1,0:T(8,128)(2,1)} %constant.96.clone.table_hbm), custom_call_target="tpu_custom_call" | custom-call | tf_op jit(solution)/shard_map/pallas_call | solution.py:401
  67.4 0.0 copy-start
  67.4 0.0 copy-start.1
  67.4 54.3 %all_to_all.11 = f32[64,120,128]{2,1,0:T(8,128)S(1)} all-to-all(f32[64,120,128]{2,1,0:T(8,128)S(1)} %bitcast.16), channel_id=1, replica_groups=mesh['row'=16,'z'=4,'core'=2] {'row','z'}, dimensions={0} | all-to-all | bytes 7864320 | tf_op jit(solution)/shard_map/all_to_all | solution.py:456
  121.7 0.0 copy-done
  121.7 0.0 copy-done.1
  121.7 4.3 %shard_map.75 = f32[8,3,320,128]{3,2,1,0:T(8,128)} custom-call(f32[7680,128]{1,0:T(8,128)S(1)} %bitcast.17, bf16[320,960]{1,0:T(8,128)(2,1)S(1)} %copy-done.1, bf16[320,960]{1,0:T(8,128)(2,1)S(1)} %copy-done), custom_call_target="tpu_custom_call" | custom-call | tf_op jit(solution)/shard_map/pallas_call | solution.py:421
  (4 shorter events, 0.0 us)
Async XLA Ops:
  4.8 39.2 %copy-start.2 = (f32[8,384]{1,0:T(8,128)S(1)}, f32[8,384]{1,0:T(8,128)}, u32[]{:S(2)}) copy-start(f32[8,384]{1,0:T(8,128)} %constant.95.clone.swap_ref) | copy-start | bytes 36868
  40.5 3.4 %collective-permute-start = (f32[64,48,128]{2,1,0:T(8,128)S(1)}, f32[64,48,128]{2,1,0:T(8,128)S(1)}, u32[]{:S(2)}, u32[]{:S(2)}) collective-permute-start(f32[64,48,128]{2,1,0:T(8,128)S(1)} %all_to_all.10), channel_id=1, source_target_pairs={{0,1},{1,0},{2,3},{3,2},{4,5},{5,4},{6,7},{7,6},{8,9},{9,8},{10,11... | collective-permute-start | bytes 4718600 | tf_op jit(solution)/shard_map/ppermute | solution.py:452
  67.4 54.3 %copy-start = (bf16[320,960]{1,0:T(8,128)(2,1)S(1)}, bf16[320,960]{1,0:T(8,128)(2,1)}, u32[]{:S(2)}) copy-start(bf16[320,960]{1,0:T(8,128)(2,1)} %constant.98.clone.d5_ref) | copy-start | bytes 1843204
  67.4 54.3 %copy-start.1 = (bf16[320,960]{1,0:T(8,128)(2,1)S(1)}, bf16[320,960]{1,0:T(8,128)(2,1)}, u32[]{:S(2)}) copy-start(bf16[320,960]{1,0:T(8,128)(2,1)} %constant.97.clone.s5_ref) | copy-start | bytes 1843204

commit v5 on v4

--- a/solution.py
+++ b/solution.py
@@ -19,6 +19,7 @@
 CH = 48
 FQ = 3 * Q
 RR = 2
+SP = 4
 G = 7
 LINES = BU * BV
 EMPTY = G * 128
@@ -355,21 +356,22 @@
 
 
 def last_kernel(x_ref, s5_ref, d5_ref, out_ref):
-    k = pl.program_id(0)
+    first = pl.program_id(0) * SP
 
     def load(slot, f):
         parts = [x_ref[pl.ds((f * Q + q) * 8 + slot, CHIPS, stride=8 * FQ), :] for q in range(Q)]
         return jnp.concatenate(parts, axis=0)
 
-    for e in range(2):
-        both = rhs_split(jnp.concatenate([load(2 * k + e, 0), load(2 * k + e, 1)], axis=1))
-        y = dot(s5_ref[...], both)
-        out_ref[e, 0] = y[:, 0:128]
-        out_ref[e, 1] = y[:, 128:256]
-    both = rhs_split(jnp.concatenate([load(2 * k, 2), load(2 * k + 1, 2)], axis=1))
-    y = dot(d5_ref[...], both)
-    out_ref[0, 2] = y[:, 0:128]
-    out_ref[1, 2] = y[:, 128:256]
+    for e in range(0, SP, 2):
+        for slot in (e, e + 1):
+            both = rhs_split(jnp.concatenate([load(first + slot, 0), load(first + slot, 1)], axis=1))
+            y = dot(s5_ref[...], both)
+            out_ref[slot, 0] = y[:, 0:128]
+            out_ref[slot, 1] = y[:, 128:256]
+        both = rhs_split(jnp.concatenate([load(first + e, 2), load(first + e + 1, 2)], axis=1))
+        y = dot(d5_ref[...], both)
+        out_ref[e, 2] = y[:, 0:128]
+        out_ref[e + 1, 2] = y[:, 128:256]
 
 
 VM = pl.BlockSpec(memory_space=pltpu.VMEM)
@@ -420,10 +422,10 @@
 def last_call(x, s5, d5):
     return pl.pallas_call(
         last_kernel,
-        grid=(4,),
+        grid=(8 // SP,),
         out_shape=jax.ShapeDtypeStruct((8, 3, N, 128), F32),
         in_specs=[VM] * 3,
-        out_specs=pl.BlockSpec((2, 3, N, 128), lambda k: (k, 0, 0, 0)),
+        out_specs=pl.BlockSpec((SP, 3, N, 128), lambda k: (k, 0, 0, 0)),
         compiler_params=params(32),
     )(x, s5, d5)
 

time: 126 us -> 126 us (level)
  no operation moved by 1% of the time
where the time goes in v5:
time: 126 us
  blocking collectives  90.1 us (72%)
  Pallas kernels  32.2 us (26%)
  other arithmetic  1.93 us (2%)
  waiting for transfers between devices  1.46 us (1%)
    all_to_all x1, blocking collectives, local(): lax.all_to_all(slots.reshape(CHIPS, 8 * FQ, 128), ('row', 'z'), split_axi...  54.3 us
    all_to_all x1, blocking collectives, local(): lax.all_to_all(sent, ('row', 'z'), split_axis=0, concat_axis=0, tiled=True)  35.8 us
    pallas_call x1, Pallas kernels, middle_call(): pl.pallas_call(middle_kernel, out_shape=jax.ShapeDtypeStruct((CHIPS * 8 *...  23.4 us
    pallas_call x1, Pallas kernels, first_call(): pl.pallas_call(first_kernel, out_shape=jax.ShapeDtypeStruct((CHIPS * 48,...  4.74 us
    pallas_call x1, Pallas kernels, last_call(): pl.pallas_call(last_kernel, grid=(8 // SP,), out_shape=jax.ShapeDtypeStru...  4.08 us
  transfers between devices with their start and end apart: 1, of which 1 were waited for; matrix products, arithmetic and copies ran while one was open for 2% of the time, Pallas kernels for 0%

profile of v5, /device:TPU:0, one launch (start us, length us, event | category | flops | bytes accessed | tf_op | source)
XLA Modules:
  0.0 125.8 jit_solution(9625802461599183035)
XLA Ops:
  0.0 4.7 %shard_map.73 = f32[3072,128]{1,0:T(8,128)} custom-call(s32[1]{0:T(128)S(6)} %select_n.41.turn_ref, f32[800,320]{1,0:T(8,128)} %bitcast.21, s32[1,800]{1,0:T(1,128)} %bitcast.22, bf16[320,960]{1,0:T(8,128)(2,1)} %constant.94.clone.table_hbm), custom_call_target="tpu_custom_call" | custom-call | tf_op jit(solution)/shard_map/pallas_call | solution.py:387
  4.8 0.0 copy-start.2
  4.8 35.8 %all_to_all.10 = f32[64,48,128]{2,1,0:T(8,128)S(1)} all-to-all(f32[64,48,128]{2,1,0:T(8,128)} %bitcast.20), channel_id=1, replica_groups=mesh['row'=16,'z'=4,'core'=2] {'row','z'}, dimensions={0} | all-to-all | bytes 3145728 | tf_op jit(solution)/shard_map/all_to_all | solution.py:453
  40.5 0.0 collective-permute-start
  40.6 0.1 broadcast_add_fusion
  40.6 1.8 %fusion.4.kern_ref = f32[5,320,384]{2,1,0:T(8,128)S(1)} fusion(f32[384]{0:T(512)S(1)} %fusion.11, f32[5,320]{1,0:T(8,128)S(1)} %broadcast_add_fusion, pred[384]{0:T(512)(128)(4,1)S(1)} %iota_compare_fusion), kind=kLoop, calls=%fused_computation.6 | loop fusion | flops 4915200 | bytes 2465920 | tf_op jit(solution)/shard_map/jit(_where)/select_n | solution.py:443
  42.5 1.5 %collective-permute-done = f32[64,48,128]{2,1,0:T(8,128)S(1)} collective-permute-done((f32[64,48,128]{2,1,0:T(8,128)S(1)}, f32[64,48,128]{2,1,0:T(8,128)S(1)}, u32[]{:S(2)}, u32[]{:S(2)}) %collective-permute-start) | collective-permute-done | bytes 1572896 | tf_op jit(solution)/shard_map/ppermute | solution.py:454
  43.9 0.0 copy-done.2
  43.9 23.4 %shard_map.74 = f32[7680,128]{1,0:T(8,128)S(1)} custom-call(s32[1]{0:T(128)} %bitcast.core_ref, f32[16,4,48,128]{3,2,1,0:T(8,128)S(1)} %bitcast.18, f32[16,4,48,128]{3,2,1,0:T(8,128)S(1)} %bitcast.19, f32[5,320,384]{2,1,0:T(8,128)S(1)} %fusion.4.kern_ref, f32[8,384]{1,0:T(8,128)S(1)} %copy-done.2, bf16[9792,384]{1,0:T(8,128)(2,1)} %constant.96.clone.table_hbm), custom_call_target="tpu_custom_call" | custom-call | tf_op jit(solution)/shard_map/pallas_call | solution.py:403
  67.4 0.0 copy-start
  67.4 0.0 copy-start.1
  67.4 54.3 %all_to_all.11 = f32[64,120,128]{2,1,0:T(8,128)S(1)} all-to-all(f32[64,120,128]{2,1,0:T(8,128)S(1)} %bitcast.16), channel_id=1, replica_groups=mesh['row'=16,'z'=4,'core'=2] {'row','z'}, dimensions={0} | all-to-all | bytes 7864320 | tf_op jit(solution)/shard_map/all_to_all | solution.py:458
  121.7 0.0 copy-done
  121.7 0.0 copy-done.1
  121.7 4.1 %shard_map.75 = f32[8,3,320,128]{3,2,1,0:T(8,128)} custom-call(f32[7680,128]{1,0:T(8,128)S(1)} %bitcast.17, bf16[320,960]{1,0:T(8,128)(2,1)S(1)} %copy-done.1, bf16[320,960]{1,0:T(8,128)(2,1)S(1)} %copy-done), custom_call_target="tpu_custom_call" | custom-call | tf_op jit(solution)/shard_map/pallas_call | solution.py:423
  (4 shorter events, 0.0 us)
Async XLA Ops:
  4.8 39.2 %copy-start.2 = (f32[8,384]{1,0:T(8,128)S(1)}, f32[8,384]{1,0:T(8,128)}, u32[]{:S(2)}) copy-start(f32[8,384]{1,0:T(8,128)} %constant.95.clone.swap_ref) | copy-start | bytes 36868
  40.5 3.4 %collective-permute-start = (f32[64,48,128]{2,1,0:T(8,128)S(1)}, f32[64,48,128]{2,1,0:T(8,128)S(1)}, u32[]{:S(2)}, u32[]{:S(2)}) collective-permute-start(f32[64,48,128]{2,1,0:T(8,128)S(1)} %all_to_all.10), channel_id=1, source_target_pairs={{0,1},{1,0},{2,3},{3,2},{4,5},{5,4},{6,7},{7,6},{8,9},{9,8},{10,11... | collective-permute-start | bytes 4718600 | tf_op jit(solution)/shard_map/ppermute | solution.py:454
  67.4 54.3 %copy-start = (bf16[320,960]{1,0:T(8,128)(2,1)S(1)}, bf16[320,960]{1,0:T(8,128)(2,1)}, u32[]{:S(2)}) copy-start(bf16[320,960]{1,0:T(8,128)(2,1)} %constant.98.clone.d5_ref) | copy-start | bytes 1843204
  67.4 54.3 %copy-start.1 = (bf16[320,960]{1,0:T(8,128)(2,1)S(1)}, bf16[320,960]{1,0:T(8,128)(2,1)}, u32[]{:S(2)}) copy-start(bf16[320,960]{1,0:T(8,128)(2,1)} %constant.97.clone.s5_ref) | copy-start | bytes 1843204

commit v6 on v5

--- a/solution.py
+++ b/solution.py
@@ -234,6 +234,15 @@
     mine = core == 0
     lane = lax.broadcasted_iota(jnp.int32, (1, 128), 1)
 
+    def sort_codes(r, carry):
+        for zc in range(8):
+            z, c = zc // 2, zc % 2
+            blk = jnp.where(core == c, own_ref[r, z, 40:48, :], oth_ref[r, z, 40:48, :])
+            code_ref[pl.ds(r * 32 + zc, 4, stride=8), :] = jnp.where(mine, blk[0:4], blk[4:8]).astype(jnp.int32)
+        return carry
+
+    lax.fori_loop(0, ROWS, sort_codes, 0)
+
     pieces = []
     for z in range(ZS):
         a = own_ref[:, z, 0:40, :].reshape(ROWS * 40, 128)
@@ -283,15 +292,6 @@
         for k, q in enumerate(pair):
             keep(0, q, y[:, k * 384 : (k + 1) * 384])
 
-    def sort_codes(r, carry):
-        for zc in range(8):
-            z, c = zc // 2, zc % 2
-            blk = jnp.where(core == c, own_ref[r, z, 40:48, :], oth_ref[r, z, 40:48, :])
-            code_ref[pl.ds(r * 32 + zc, 4, stride=8), :] = jnp.where(mine, blk[0:4], blk[4:8]).astype(jnp.int32)
-        return carry
-
-    lax.fori_loop(0, ROWS, sort_codes, 0)
-
     def lines_of(k, ref):
         at = pl.ds(pl.multiple_of(k * RR * 8, RR * 8), RR * 8)
         ys = []

time: 126 us -> 126 us (level)
  no operation moved by 1% of the time
where the time goes in v6:
time: 126 us
  blocking collectives  90.1 us (72%)
  Pallas kernels  32.1 us (25%)
  other arithmetic  1.93 us (2%)
  waiting for transfers between devices  1.46 us (1%)
    all_to_all x1, blocking collectives, local(): lax.all_to_all(slots.reshape(CHIPS, 8 * FQ, 128), ('row', 'z'), split_axi...  54.4 us
    all_to_all x1, blocking collectives, local(): lax.all_to_all(sent, ('row', 'z'), split_axis=0, concat_axis=0, tiled=True)  35.8 us
    pallas_call x1, Pallas kernels, middle_call(): pl.pallas_call(middle_kernel, out_shape=jax.ShapeDtypeStruct((CHIPS * 8 *...  23.2 us
    pallas_call x1, Pallas kernels, first_call(): pl.pallas_call(first_kernel, out_shape=jax.ShapeDtypeStruct((CHIPS * 48,...  4.74 us
    pallas_call x1, Pallas kernels, last_call(): pl.pallas_call(last_kernel, grid=(8 // SP,), out_shape=jax.ShapeDtypeStru...  4.08 us
  transfers between devices with their start and end apart: 1, of which 1 were waited for; matrix products, arithmetic and copies ran while one was open for 2% of the time, Pallas kernels for 0%

profile of v6, /device:TPU:0, one launch (start us, length us, event | category | flops | bytes accessed | tf_op | source)
XLA Modules:
  0.0 125.6 jit_solution(7391640862716194188)
XLA Ops:
  0.0 4.7 %shard_map.73 = f32[3072,128]{1,0:T(8,128)} custom-call(s32[1]{0:T(128)S(6)} %select_n.41.turn_ref, f32[800,320]{1,0:T(8,128)} %bitcast.21, s32[1,800]{1,0:T(1,128)} %bitcast.22, bf16[320,960]{1,0:T(8,128)(2,1)} %constant.94.clone.table_hbm), custom_call_target="tpu_custom_call" | custom-call | tf_op jit(solution)/shard_map/pallas_call | solution.py:387
  4.8 0.0 copy-start.2
  4.8 35.8 %all_to_all.10 = f32[64,48,128]{2,1,0:T(8,128)S(1)} all-to-all(f32[64,48,128]{2,1,0:T(8,128)} %bitcast.20), channel_id=1, replica_groups=mesh['row'=16,'z'=4,'core'=2] {'row','z'}, dimensions={0} | all-to-all | bytes 3145728 | tf_op jit(solution)/shard_map/all_to_all | solution.py:453
  40.5 0.0 collective-permute-start
  40.6 0.1 broadcast_add_fusion
  40.6 1.8 %fusion.4.kern_ref = f32[5,320,384]{2,1,0:T(8,128)S(1)} fusion(f32[384]{0:T(512)S(1)} %fusion.11, f32[5,320]{1,0:T(8,128)S(1)} %broadcast_add_fusion, pred[384]{0:T(512)(128)(4,1)S(1)} %iota_compare_fusion), kind=kLoop, calls=%fused_computation.6 | loop fusion | flops 4915200 | bytes 2465920 | tf_op jit(solution)/shard_map/jit(_where)/select_n | solution.py:443
  42.5 1.5 %collective-permute-done = f32[64,48,128]{2,1,0:T(8,128)S(1)} collective-permute-done((f32[64,48,128]{2,1,0:T(8,128)S(1)}, f32[64,48,128]{2,1,0:T(8,128)S(1)}, u32[]{:S(2)}, u32[]{:S(2)}) %collective-permute-start) | collective-permute-done | bytes 1572896 | tf_op jit(solution)/shard_map/ppermute | solution.py:454
  43.9 0.0 copy-done.2
  43.9 23.2 %shard_map.74 = f32[7680,128]{1,0:T(8,128)S(1)} custom-call(s32[1]{0:T(128)} %bitcast.core_ref, f32[16,4,48,128]{3,2,1,0:T(8,128)S(1)} %bitcast.18, f32[16,4,48,128]{3,2,1,0:T(8,128)S(1)} %bitcast.19, f32[5,320,384]{2,1,0:T(8,128)S(1)} %fusion.4.kern_ref, f32[8,384]{1,0:T(8,128)S(1)} %copy-done.2, bf16[9792,384]{1,0:T(8,128)(2,1)} %constant.96.clone.table_hbm), custom_call_target="tpu_custom_call" | custom-call | tf_op jit(solution)/shard_map/pallas_call | solution.py:403
  67.2 0.0 copy-start
  67.2 0.0 copy-start.1
  67.2 54.4 %all_to_all.11 = f32[64,120,128]{2,1,0:T(8,128)S(1)} all-to-all(f32[64,120,128]{2,1,0:T(8,128)S(1)} %bitcast.16), channel_id=1, replica_groups=mesh['row'=16,'z'=4,'core'=2] {'row','z'}, dimensions={0} | all-to-all | bytes 7864320 | tf_op jit(solution)/shard_map/all_to_all | solution.py:458
  121.5 0.0 copy-done
  121.5 0.0 copy-done.1
  121.5 4.1 %shard_map.75 = f32[8,3,320,128]{3,2,1,0:T(8,128)} custom-call(f32[7680,128]{1,0:T(8,128)S(1)} %bitcast.17, bf16[320,960]{1,0:T(8,128)(2,1)S(1)} %copy-done.1, bf16[320,960]{1,0:T(8,128)(2,1)S(1)} %copy-done), custom_call_target="tpu_custom_call" | custom-call | tf_op jit(solution)/shard_map/pallas_call | solution.py:423
  (4 shorter events, 0.0 us)
Async XLA Ops:
  4.8 39.2 %copy-start.2 = (f32[8,384]{1,0:T(8,128)S(1)}, f32[8,384]{1,0:T(8,128)}, u32[]{:S(2)}) copy-start(f32[8,384]{1,0:T(8,128)} %constant.95.clone.swap_ref) | copy-start | bytes 36868
  40.5 3.4 %collective-permute-start = (f32[64,48,128]{2,1,0:T(8,128)S(1)}, f32[64,48,128]{2,1,0:T(8,128)S(1)}, u32[]{:S(2)}, u32[]{:S(2)}) collective-permute-start(f32[64,48,128]{2,1,0:T(8,128)S(1)} %all_to_all.10), channel_id=1, source_target_pairs={{0,1},{1,0},{2,3},{3,2},{4,5},{5,4},{6,7},{7,6},{8,9},{9,8},{10,11... | collective-permute-start | bytes 4718600 | tf_op jit(solution)/shard_map/ppermute | solution.py:454
  67.2 54.4 %copy-start = (bf16[320,960]{1,0:T(8,128)(2,1)S(1)}, bf16[320,960]{1,0:T(8,128)(2,1)}, u32[]{:S(2)}) copy-start(bf16[320,960]{1,0:T(8,128)(2,1)} %constant.98.clone.d5_ref) | copy-start | bytes 1843204
  67.2 54.4 %copy-start.1 = (bf16[320,960]{1,0:T(8,128)(2,1)S(1)}, bf16[320,960]{1,0:T(8,128)(2,1)}, u32[]{:S(2)}) copy-start(bf16[320,960]{1,0:T(8,128)(2,1)} %constant.97.clone.s5_ref) | copy-start | bytes 1843204
